TPU v7x, 512 devices: a whole 4x4x16 slice. The times are simulated.
512 devices in a mesh: lat: 32 (over z, core), ens: 16 (over x, y).
Axes of the slice: x: 4, y: 4, z: 16, core: 2. Of those that a mesh axis runs over, the one named last changes fastest.
Arguments:
- inputs: bfloat16 [16, 32, 720, 256], P('ens', 'lat'), may hold values from -6 to 6
- cotangent: bfloat16 [16, 32, 720, 256], P('ens', 'lat'), may hold values from -6 to 6
- weights: bfloat16 [4, 256, 256], replicated, may hold values from -0.1875 to 0.1875
- cycle_offsets: int32 [32, 16], P('lat'), may hold values from -1 to 1
- lon_shifts: int32 [32, 16], P('lat'), may hold values from 0 to 719
- basis_ids: int32 [32, 16], P('lat'), may hold values from 0 to 3
- entry_values: bfloat16 [32, 16], P('lat'), may hold values from 0.099609375 to 1
Outputs:
- activations: bfloat16 [16, 32, 720, 256], P('ens', 'lat')
- grad_inputs: bfloat16 [16, 32, 720, 256], P('ens', 'lat')
- grad_weights: float32 [4, 256, 256], replicated
Inputs may be any that keep to these rules, and one draw needn't show every extreme that they name: `cycle_offsets`: an entry's cycle lies at most 1 cycle from its output cycle.
All inputs are finite; a program needn't handle non-finite values.
Results may differ from a plain program's by a relative error of at most 0.0063.
Values may be sent and summed in bfloat16 or wider, within the bound.
No kernel may reach another device: no remote copies, remote signals or barrier semaphores. Data moves between devices by JAX's collectives and lax.ppermute only.
A program may use at most 192 MiB of HBM per device.

v0:
```python
import math

import jax
import jax.numpy as jnp
from jax import lax
from jax.sharding import PartitionSpec as P

H = 1


def with_halo(cells, sides, width):
    for axis, dim in sides:
        count = lax.axis_size(axis)
        ends = count - 1
        head = lax.slice_in_dim(cells, 0, width, axis=dim)
        tail = lax.slice_in_dim(cells, cells.shape[dim] - width, cells.shape[dim], axis=dim)
        cells = jnp.concatenate(
            [
                lax.ppermute(tail, axis, [(i, (i + 1) % count) for i in range(ends)]),
                cells,
                lax.ppermute(head, axis, [((i + 1) % count, i) for i in range(ends)]),
            ],
            axis=dim,
        )
    return cells


def passed_along(block, axis, distance):
    devices = range(lax.axis_size(axis))
    route = [(i - distance, i) for i in devices if i - distance in devices]
    return lax.ppermute(block, axis, route)


def basis_forward(padded, offsets, shifts, basis_of_all, entry_coefs, basis_count, group_size):
    cycle_count, entry_count = offsets.shape
    lon_count = padded.shape[1]
    channels = padded.shape[2]
    margin = (padded.shape[0] - cycle_count) // 2
    cycle_block = max(1, group_size // entry_count)
    turn_count = cycle_count * entry_count // group_size
    owners = jnp.arange(cycle_count * entry_count, dtype=jnp.int32) // entry_count
    flat_offsets = offsets.reshape(-1)
    flat_shifts = shifts.reshape(-1)
    flat_basis = basis_of_all.reshape(-1)
    flat_coefs = entry_coefs.reshape(-1)
    lon_index = jnp.arange(lon_count, dtype=jnp.int32)
    basis_index = jnp.arange(basis_count, dtype=jnp.int32)
    slot_index = jnp.arange(cycle_block, dtype=jnp.int32)

    def step_forward(counter, summed):
        start_entry = counter * group_size
        first_cycle = start_entry // entry_count
        source = owners + margin + flat_offsets
        columns = (lon_index[None, :] + flat_shifts[:, None]) % lon_count
        latitude_slab_rows = padded[source[:, None], columns]
        chosen = ((owners - first_cycle)[:, None] == slot_index[None, :])[:, :, None] & (
            flat_basis[:, None] == basis_index[None, :]
        )[:, None, :]
        channel_mixing = jnp.where(chosen, flat_coefs[:, None, None], jnp.zeros((), jnp.bfloat16))
        partial_value = jnp.einsum(
            "nzw,naq->zawq", channel_mixing, latitude_slab_rows, preferred_element_type=jnp.float32
        )
        return summed + partial_value

    start = jnp.zeros((cycle_count, lon_count, basis_count, channels), jnp.float32)
    return lax.fori_loop(0, turn_count, step_forward, start)


def basis_backward(grad_basis, offsets, shifts, basis_of_all, entry_coefs, margin, group_size):
    cycle_count, entry_count = offsets.shape
    lon_count = grad_basis.shape[1]
    channels = grad_basis.shape[3]
    cycle_block = max(1, group_size // entry_count)
    span_cycles = cycle_block + 2 * margin
    turn_count = cycle_count * entry_count // group_size
    owners = jnp.arange(cycle_count * entry_count, dtype=jnp.int32) // entry_count
    flat_offsets = offsets.reshape(-1)
    flat_shifts = shifts.reshape(-1)
    flat_basis = basis_of_all.reshape(-1)
    flat_coefs = entry_coefs.reshape(-1)
    lon_index = jnp.arange(lon_count, dtype=jnp.int32)
    target_positions = jnp.arange(span_cycles, dtype=jnp.int32)

    def step_forward(counter, summed):
        start_entry = counter * group_size
        first_cycle = start_entry // entry_count
        target = owners - first_cycle + margin + flat_offsets
        columns = (lon_index[None, :] - flat_shifts[:, None]) % lon_count
        latitude_slab_rows = grad_basis[owners[:, None], columns, flat_basis[:, None]]
        channel_mixing = jnp.where(
            target[:, None] == target_positions[None, :],
            flat_coefs[:, None],
            jnp.zeros((), jnp.bfloat16),
        )
        partial_value = jnp.einsum(
            "ys,yej->sej", channel_mixing, latitude_slab_rows, preferred_element_type=jnp.float32
        )
        return summed + partial_value

    start = jnp.zeros((cycle_count + 2 * margin, lon_count, channels), jnp.float32)
    return lax.fori_loop(0, turn_count, step_forward, start)


def on_device(inputs, cotangent, weights, cycle_offsets, lon_shifts, basis_ids, entry_values):
    field_now = inputs[0]
    grad_now = cotangent[0]
    cycle_count, lon_count, channels = field_now.shape
    basis_count = weights.shape[0]
    entry_count = cycle_offsets.shape[1]
    lat_count = lax.axis_size("lat")
    padded = with_halo(field_now, (("lat", 0),), H)
    basis_out = basis_forward(
        padded, cycle_offsets, lon_shifts, basis_ids, entry_values, basis_count, entry_count
    ).astype(jnp.bfloat16)
    flat_basis = basis_out.reshape(cycle_count * lon_count, basis_count * channels)
    flat_weights = weights.reshape(basis_count * channels, channels)
    preact = jnp.dot(flat_basis, flat_weights, preferred_element_type=jnp.float32)
    activated, gelu_back = jax.vjp(jax.nn.gelu, preact)
    grad_pre = gelu_back(grad_now.reshape(cycle_count * lon_count, channels).astype(jnp.float32))[
        0
    ].astype(jnp.bfloat16)
    product = lax.dot_general(
        grad_pre, flat_weights, (((1,), (1,)), ((), ())), preferred_element_type=jnp.float32
    )
    grad_basis = product.astype(jnp.bfloat16).reshape(-1, lon_count, basis_count, channels)
    partial_w = lax.dot_general(
        flat_basis, grad_pre, (((0,), (0,)), ((), ())), preferred_element_type=jnp.float32
    )
    back_sum = basis_backward(
        grad_basis, cycle_offsets, lon_shifts, basis_ids, entry_values, H, entry_count
    )
    from_above = passed_along(back_sum[cycle_count + H :], "lat", 1)
    from_below = passed_along(back_sum[:H], "lat", -1)
    core_cycles = back_sum[H : H + cycle_count]
    core_cycles = core_cycles.at[:H].add(from_above)
    core_cycles = core_cycles.at[cycle_count - H :].add(from_below)
    field_gradient = core_cycles.astype(jnp.bfloat16)
    summed_w = lax.psum(partial_w, ("lat", "ens"))
    cell_count = lax.axis_size("ens") * lat_count * cycle_count * lon_count
    grad_weights = (summed_w * (1.0 / math.sqrt(cell_count))).reshape(
        basis_count, channels, channels
    )
    activations = activated.astype(jnp.bfloat16).reshape(1, cycle_count, lon_count, channels)
    return (activations, field_gradient[None], grad_weights)


def solution(mesh):
    placed = (
        P("ens", "lat", None, None),
        P("ens", "lat", None, None),
        P(),
        P("lat", None),
        P("lat", None),
        P("lat", None),
        P("lat", None),
    )
    return jax.shard_map(
        on_device,
        mesh=mesh,
        in_specs=placed,
        out_specs=(P("ens", "lat", None, None), P("ens", "lat", None, None), P()),
        check_vma=False,
    )
```

profile of v0, /device:TPU:1, one launch (start us, length us, event | category | flops | bytes accessed | tf_op | source)
XLA Modules:
  0.0 601.3 jit_solution(17889327225152244846)
XLA Ops:
  7.2 8.9 %collective-permute-start.1 = (bf16[1,720,256]{2,1,0:T(8,128)(2,1)}, bf16[1,720,256]{2,1,0:T(8,128)(2,1)S(1)}, u32[]{:S(2)}, u32[]{:S(2)}) collective-permute-start(bf16[1,720,256]{2,1,0:T(8,128)(2,1)} %bitcast.51), channel_id=1, source_target_pairs={{16,0},{32,16},{48,32},{64,48},{80,64},{96,80},{112,96},{128,112},... | collective-permute-start | bytes 1105928 | tf_op jit(solution)/shard_map/ppermute | solution.py:21
  16.2 1.9 collective-permute-start
  18.1 0.7 add_add_fusion
  18.7 0.7 fusion.48
  19.4 0.8 fusion.26
  20.4 2.4 collective-permute-done
  22.8 1.1 pad_maximum_fusion
  24.0 86.6 %gather_fusion = bf16[11520,256]{1,0:T(8,128)(2,1)} fusion(bf16[3,720,256]{2,1,0:T(8,128)(2,1)S(1)} %pad_maximum_fusion, s32[11520]{0:T(1024)S(1)} %reshape.339), kind=kCustom, calls=%fused_computation | custom fusion | bytes 11888640 | tf_op jit(solution)/shard_map/while/body/eval_jaxpr/gather | solution.py:55
  110.6 4.7 fusion.4
  115.3 0.3 copy.15
  115.6 0.5 fusion.59
  116.2 2.0 fusion.55
  118.2 0.9 convolution_convert_fusion
  119.1 1.2 reshape.336
  120.3 86.2 %gather_fusion.1 = bf16[11520,256]{1,0:T(8,128)(2,1)} fusion(bf16[1,720,4,256]{3,2,1,0:T(4,128)(2,1)S(1)} %reshape.336, s32[11520]{0:T(1024)S(1)} %reshape.345), kind=kCustom, calls=%fused_computation.1 | custom fusion | bytes 11934720 | tf_op jit(solution)/shard_map/while/body/eval_jaxpr/gather | solution.py:89
  206.5 4.7 fusion
  211.2 2.3 fusion.58
  213.5 4.3 collective-permute-start.2
  217.7 1.9 collective-permute-start.3
  219.7 1.0 fusion.19
  220.6 368.0 %all-reduce.2.cloned.1.call-done = f32[1024,256]{1,0:T(8,128)} async-done(((f32[1024,256]{1,0:T(8,128)}), f32[1024,256]{1,0:T(8,128)}) %all-reduce.2.cloned.1.call-update) | async-done | bytes 1048592 | tf_op jit(solution)/shard_map/psum | solution.py:138
  588.6 2.3 broadcast_multiply_fusion
  590.9 2.8 fusion.18
  593.7 0.8 copy.23
  (20 shorter events, 0.3 us)
Async XLA Ops:
  7.2 108.5 %copy-start = (bf16[4,256,256]{2,1,0:T(8,128)(2,1)S(1)}, bf16[4,256,256]{2,1,0:T(8,128)(2,1)}, u32[]{:S(2)}) copy-start(bf16[4,256,256]{2,1,0:T(8,128)(2,1)} %param.17) | copy-start | bytes 1572868
  7.2 581.4 %all-reduce.2.cloned.1.call-start = ((), (), s32[]{:S(2)}) async-start(), calls=%async_computation | async-start | bytes 2097152 | tf_op jit(solution)/shard_map/psum | solution.py:138
  7.2 13.2 %collective-permute-start.1 = (bf16[1,720,256]{2,1,0:T(8,128)(2,1)}, bf16[1,720,256]{2,1,0:T(8,128)(2,1)S(1)}, u32[]{:S(2)}, u32[]{:S(2)}) collective-permute-start(bf16[1,720,256]{2,1,0:T(8,128)(2,1)} %bitcast.51), channel_id=1, source_target_pairs={{16,0},{32,16},{48,32},{64,48},{80,64},{96,80},{112,96},{128,112},... | collective-permute-start | bytes 1105928 | tf_op jit(solution)/shard_map/ppermute | solution.py:21
  16.2 6.7 %collective-permute-start = (bf16[1,720,256]{2,1,0:T(8,128)(2,1)}, bf16[1,720,256]{2,1,0:T(8,128)(2,1)S(1)}, u32[]{:S(2)}, u32[]{:S(2)}) collective-permute-start(bf16[1,720,256]{2,1,0:T(8,128)(2,1)} %bitcast.52), channel_id=1, source_target_pairs={{0,16},{16,32},{32,48},{48,64},{64,80},{80,96},{96,112},{112,128},... | collective-permute-start | bytes 1105928 | tf_op jit(solution)/shard_map/ppermute | solution.py:19
  23.9 86.6 %copy-start.3 = (bf16[1,16]{1,0:T(2,128)(2,1)S(1)}, bf16[1,16]{1,0:T(2,128)(2,1)}, u32[]{:S(2)}) copy-start(bf16[1,16]{1,0:T(2,128)(2,1)} %param.21) | copy-start | bytes 100
  24.0 86.6 %copy-start.5 = (s32[1,16]{1,0:T(1,128)S(1)}, s32[1,16]{1,0:T(1,128)}, u32[]{:S(2)}) copy-start(s32[1,16]{1,0:T(1,128)} %param.20) | copy-start | bytes 196
  110.6 5.6 copy-start.4
  116.2 2.9 copy-start.1
  206.5 13.2 %copy-start.2 = (f32[720,256]{1,0:T(8,128)S(1)}, f32[720,256]{1,0:T(8,128)}, u32[]{:S(2)}) copy-start(f32[720,256]{1,0:T(8,128)} %copy-done.1) | copy-start | bytes 2211844
  213.5 377.4 %collective-permute-start.2 = (f32[1,720,256]{2,0,1:T(1,128)}, f32[1,720,256]{2,0,1:T(1,128)}, u32[]{:S(2)}, u32[]{:S(2)}) collective-permute-start(f32[1,720,256]{2,0,1:T(1,128)} %get-tuple-element.109), channel_id=1, source_target_pairs={{0,16},{16,32},{32,48},{48,64},{64,80},{80,96},{96,112},{112,128},... | collective-permute-start | bytes 2211848 | tf_op jit(solution)/shard_map/ppermute | solution.py:31
  217.7 373.2 %collective-permute-start.3 = (f32[1,720,256]{2,0,1:T(1,128)}, f32[1,720,256]{2,0,1:T(1,128)}, u32[]{:S(2)}, u32[]{:S(2)}) collective-permute-start(f32[1,720,256]{2,0,1:T(1,128)} %get-tuple-element.110), channel_id=1, source_target_pairs={{16,0},{32,16},{48,32},{64,48},{80,64},{96,80},{112,96},{128,112},... | collective-permute-start | bytes 2211848 | tf_op jit(solution)/shard_map/ppermute | solution.py:31
Sparse Core Ops, SparseCore 0:
  119.3 469.2 all-reduce.1
where the time goes:
time: 602 us; the launch traced here: 601 us
  waiting for transfers between devices  370 us (61%)
  local copies, waits for them, and re-layouts  178 us (30%)
  starting transfers between devices  17.1 us (3%)
  between operations  14.2 us (2%)
  matrix products  12.9 us (2%)
  other arithmetic  9.33 us (2%)
    psum x1, waiting for transfers between devices, on_device(): summed_w = lax.psum(partial_w, ('lat', 'ens'))  368 us
    gather x1, local copies, waits for them, and re-layouts, step_forward(): latitude_slab_rows = padded[source[:, None], columns]  86.6 us
    gather x1, local copies, waits for them, and re-layouts, step_forward(): grad_basis[owners[:, None], columns, flat_basis[:, None]]  86.2 us
  transfers between devices with their start and end apart: 5, of which 2 were waited for; matrix products, arithmetic and copies ran while one was open for 17% of the time, Pallas kernels for 0%

commit v1 on v0

v1 whole, which is shorter than its diff:
```python
import functools
import math

import jax
import jax.numpy as jnp
import numpy as np
from jax import lax
from jax.experimental import pallas as pl
from jax.experimental.pallas import tpu as pltpu
from jax.sharding import Mesh
from jax.sharding import PartitionSpec as P

BF16 = jnp.bfloat16
F32 = jnp.float32
LANES = 128
SLAB = 48
VMEM_BYTES = 48 * 1024 * 1024
LAT = ("za", "zp", "core")
ENS = ("x", "y")
NEAR = ("zp", "core", "x", "y")
FAR = ("za",)


def along(axis, distance):
    devices = range(lax.axis_size(axis))
    return [(i - distance, i) for i in devices if i - distance in devices]


def fill_twice(slabs, slot, field):
    lon_count = field.shape[0]
    for half in range(field.shape[1] // LANES):
        part = field[:, half * LANES : (half + 1) * LANES]
        slabs[slot + half, 0:lon_count, :] = part
        slabs[slot + half, lon_count : 2 * lon_count, :] = part


def forward_kernel(
    offsets, shifts, basis_ids, values, below, own, above, weights, cotangent,
    activated, grad_pre, partial_w, slabs, summed, basis, preact,
):
    lon_count, channels = own.shape
    halves = channels // LANES
    basis_count = weights.shape[0] // channels
    for slot, field in enumerate((below, own, above)):
        fill_twice(slabs, slot * halves, field[...].astype(F32))
    summed[...] = jnp.zeros_like(summed)

    def add_entry(entry, carry):
        source = (offsets[0, entry] + 1) * halves
        target = basis_ids[0, entry] * halves
        shift = shifts[0, entry]
        value = values[0, entry]
        for half in range(halves):
            summed[target + half] += value * slabs[source + half, pl.ds(shift, lon_count), :]
        return carry

    lax.fori_loop(0, offsets.shape[1], add_entry, 0)
    for column in range(basis_count * halves):
        basis[:, column * LANES : (column + 1) * LANES] = summed[column].astype(BF16)
    preact[...] = jnp.dot(basis[...], weights[...], preferred_element_type=F32)

    def gelu_rows(step, carry):
        rows = pl.ds(pl.multiple_of(step * SLAB, SLAB), SLAB)
        v = preact[rows, :]
        root = math.sqrt(2.0 / math.pi)
        square = v * v
        bent = jnp.tanh(root * (v + 0.044715 * (v * square)))
        activated[rows, :] = (0.5 * v * (1.0 + bent)).astype(BF16)
        slope = 0.5 * (1.0 + bent) + 0.5 * v * (1.0 - bent * bent) * (
            root * (1.0 + (3.0 * 0.044715) * square)
        )
        grad_pre[rows, :] = (cotangent[rows, :].astype(F32) * slope).astype(BF16)
        return carry

    lax.fori_loop(0, lon_count // SLAB, gelu_rows, 0)
    partial_w[...] = lax.dot_general(
        basis[...], grad_pre[...], (((0,), (0,)), ((), ())), preferred_element_type=F32
    ).astype(BF16)


def backward_kernel(
    offsets, shifts, basis_ids, values, grad_pre, weights, down, own, up, slabs, summed,
):
    lon_count, channels = grad_pre.shape
    halves = channels // LANES
    basis_count = weights.shape[0] // channels
    for k in range(basis_count):
        product = lax.dot_general(
            grad_pre[...],
            weights[k * channels : (k + 1) * channels, :],
            (((1,), (1,)), ((), ())),
            preferred_element_type=F32,
        )
        fill_twice(slabs, k * halves, product.astype(BF16).astype(F32))
    summed[...] = jnp.zeros_like(summed)

    def add_entry(entry, carry):
        target = (offsets[0, entry] + 1) * halves
        source = basis_ids[0, entry] * halves
        start = lon_count - shifts[0, entry]
        value = values[0, entry]
        for half in range(halves):
            summed[target + half] += value * slabs[source + half, pl.ds(start, lon_count), :]
        return carry

    lax.fori_loop(0, offsets.shape[1], add_entry, 0)
    for slot, out in enumerate((down, own, up)):
        for half in range(halves):
            out[:, half * LANES : (half + 1) * LANES] = summed[slot * halves + half].astype(out.dtype)


def specs(scalars, arrays):
    return [pl.BlockSpec(memory_space=pltpu.SMEM)] * scalars + [
        pl.BlockSpec(memory_space=pltpu.VMEM)
    ] * arrays


def forward(tables, below, own, above, weights, cotangent):
    lon_count, channels = own.shape
    halves = channels // LANES
    wide = weights.shape[0]
    return pl.pallas_call(
        forward_kernel,
        out_shape=(
            jax.ShapeDtypeStruct((lon_count, channels), BF16),
            jax.ShapeDtypeStruct((lon_count, channels), BF16),
            jax.ShapeDtypeStruct((wide, channels), BF16),
        ),
        in_specs=specs(4, 5),
        out_specs=tuple(specs(0, 3)),
        scratch_shapes=[
            pltpu.VMEM((3 * halves, 2 * lon_count, LANES), F32),
            pltpu.VMEM((wide // LANES, lon_count, LANES), F32),
            pltpu.VMEM((lon_count, wide), BF16),
            pltpu.VMEM((lon_count, channels), F32),
        ],
        compiler_params=pltpu.CompilerParams(vmem_limit_bytes=VMEM_BYTES),
        cost_estimate=pl.CostEstimate(
            flops=4 * lon_count * wide * channels, bytes_accessed=16 * 1024 * 1024, transcendentals=0
        ),
        name="conv_forward",
    )(*tables, below, own, above, weights, cotangent)


def backward(tables, grad_pre, weights):
    lon_count, channels = grad_pre.shape
    halves = channels // LANES
    wide = weights.shape[0]
    return pl.pallas_call(
        backward_kernel,
        out_shape=(
            jax.ShapeDtypeStruct((lon_count, channels), BF16),
            jax.ShapeDtypeStruct((lon_count, channels), F32),
            jax.ShapeDtypeStruct((lon_count, channels), BF16),
        ),
        in_specs=specs(4, 2),
        out_specs=tuple(specs(0, 3)),
        scratch_shapes=[
            pltpu.VMEM((wide // LANES, 2 * lon_count, LANES), F32),
            pltpu.VMEM((3 * halves, lon_count, LANES), F32),
        ],
        compiler_params=pltpu.CompilerParams(vmem_limit_bytes=VMEM_BYTES),
        cost_estimate=pl.CostEstimate(
            flops=2 * lon_count * wide * channels, bytes_accessed=16 * 1024 * 1024, transcendentals=0
        ),
        name="conv_backward",
    )(*tables, grad_pre, weights)


def gathered(block, axes):
    count = lax.axis_size(axes)
    return lax.all_to_all(jnp.broadcast_to(block[None], (count,) + block.shape), axes, 0, 0)


def on_device(inputs, cotangent, weights, cycle_offsets, lon_shifts, basis_ids, entry_values):
    own = inputs[0, 0]
    lon_count, channels = own.shape
    basis_count = weights.shape[0]
    flat_weights = weights.reshape(basis_count * channels, channels)
    tables = (cycle_offsets, lon_shifts, basis_ids, entry_values.astype(F32))
    below = lax.ppermute(own, LAT, along(LAT, 1))
    above = lax.ppermute(own, LAT, along(LAT, -1))
    activated, grad_pre, partial_w = forward(
        tables, below, own, above, flat_weights, cotangent[0, 0]
    )
    near = lax.axis_size(NEAR)
    pieces = lax.all_to_all(partial_w.reshape(near, -1, channels), NEAR, 0, 0)
    chunk = pieces.astype(F32).sum(0).astype(BF16)

    down, middle, up = backward(tables, grad_pre, flat_weights)
    from_above = lax.ppermute(up, LAT, along(LAT, 1))
    from_below = lax.ppermute(down, LAT, along(LAT, -1))
    field_gradient = (middle + from_above.astype(F32) + from_below.astype(F32)).astype(BF16)

    cell_count = lax.axis_size(LAT) * lax.axis_size(ENS) * lon_count
    total = gathered(chunk, FAR).astype(F32).sum(0) * (1.0 / math.sqrt(cell_count))
    whole = gathered(total.astype(BF16), NEAR)
    grad_weights = whole.reshape(basis_count, channels, channels).astype(F32)
    return (activated[None, None], field_gradient[None, None], grad_weights)


def solution(mesh):
    lat_count, ens_count = mesh.devices.shape
    grid = Mesh(
        np.asarray(mesh.devices).reshape(lat_count // 4, 2, 2, 4, ens_count // 4),
        LAT + ENS,
    )
    placed = (
        P(ENS, LAT, None, None),
        P(ENS, LAT, None, None),
        P(),
        P(LAT, None),
        P(LAT, None),
        P(LAT, None),
        P(LAT, None),
    )
    return jax.shard_map(
        on_device,
        mesh=grid,
        in_specs=placed,
        out_specs=(P(ENS, LAT, None, None), P(ENS, LAT, None, None), P()),
        check_vma=False,
    )
```

time: 602 us -> 95.7 us (0.16)
  waiting for transfers between devices: 370 us -> 10.7 us
  local copies, waits for them, and re-layouts: 178 us -> 4.54 us
  blocking collectives: 0 us -> 46.4 us
  between operations: 14.2 us -> 0.75 us
  matrix products: 12.9 us -> 0 us
  Pallas kernels: 0 us -> 8.55 us
  other arithmetic: 9.33 us -> 2.05 us
    psum x1 -> x0, waiting for transfers between devices: 368 us -> none  [on_device(): summed_w = lax.psum(partial_w, ('lat', 'ens'))]
    gather x2 -> x0, local copies, waits for them, and re-layouts: 173 us -> none  [the longest x1 86.6 us: step_forward(): latitude_slab_rows = padded[source[:, None], columns]]
    all_to_all x0 -> x2, blocking collectives: none -> 46.4 us  [the longest x1 26.2 us: gathered(): lax.all_to_all(jnp.broadcast_to(block[None], (count,) + block.shape), axe...]
    dot_general x5 -> x0, matrix products: 12.9 us -> none  [the longest x1 4.73 us: step_forward(): jnp.einsum('ys,yej->sej', channel_mixing, latitude_slab_rows, preferred_e...]
    pallas_call x0 -> x2, Pallas kernels: none -> 8.55 us  [the longest x1 5.44 us: forward(): pl.pallas_call(forward_kernel, out_shape=(jax.ShapeDtypeStruct((lon_count...]
    ppermute x4, waiting for transfers between devices: 2.4 us -> 10.7 us  [the longest x1 4.4 us: on_device(): from_below = lax.ppermute(down, LAT, along(LAT, -1))]
    all_to_all x0 -> x1, starting transfers between devices: none -> 6.47 us  [gathered(): lax.all_to_all(jnp.broadcast_to(block[None], (count,) + block.shape), axe...]
  transfers between devices with their start and end apart: 5 -> 5, of which waited for: 2 -> 3; matrix products, arithmetic and copies ran while one was open for 17% -> 1% of each run, Pallas kernels for 0% -> 3%
where the time goes in v1:
time: 95.7 us; the launch traced here: 95.2 us
  blocking collectives  46.4 us (48%)
  starting transfers between devices  22.2 us (23%)
  waiting for transfers between devices  10.7 us (11%)
  Pallas kernels  8.55 us (9%)
  local copies, waits for them, and re-layouts  4.54 us (5%)
  other arithmetic  2.05 us (2%)
    all_to_all x1, blocking collectives, gathered(): lax.all_to_all(jnp.broadcast_to(block[None], (count,) + block.shape), axe...  26.2 us
    all_to_all x1, blocking collectives, on_device(): pieces = lax.all_to_all(partial_w.reshape(near, -1, channels), NEAR, 0, 0)  20.2 us
    all_to_all x1, starting transfers between devices, gathered(): lax.all_to_all(jnp.broadcast_to(block[None], (count,) + block.shape), axe...  6.47 us
    pallas_call x1, Pallas kernels, forward(): pl.pallas_call(forward_kernel, out_shape=(jax.ShapeDtypeStruct((lon_count...  5.44 us
    ppermute x1, starting transfers between devices, on_device(): above = lax.ppermute(own, LAT, along(LAT, -1))  5.17 us
    ppermute x1, starting transfers between devices, on_device(): below = lax.ppermute(own, LAT, along(LAT, 1))  4.94 us
    ppermute x1, waiting for transfers between devices, on_device(): from_below = lax.ppermute(down, LAT, along(LAT, -1))  4.4 us
    ppermute x1, waiting for transfers between devices, on_device(): above = lax.ppermute(own, LAT, along(LAT, -1))  3.84 us
  transfers between devices with their start and end apart: 5, of which 3 were waited for; matrix products, arithmetic and copies ran while one was open for 1% of the time, Pallas kernels for 3%

profile of v1, /device:TPU:1, one launch (start us, length us, event | category | flops | bytes accessed | tf_op | source)
XLA Modules:
  0.0 95.2 jit_solution(3858370996316557887)
XLA Ops:
  0.6 4.9 %collective-permute-start = (bf16[720,256]{1,0:T(8,128)(2,1)}, bf16[720,256]{1,0:T(8,128)(2,1)S(1)}, u32[]{:S(2)}, u32[]{:S(2)}) collective-permute-start(bf16[720,256]{1,0:T(8,128)(2,1)} %bitcast.14), channel_id=1, source_target_pairs={{0,16},{16,32},{32,48},{48,64},{64,80},{80,96},{96,112},{112,128},... | collective-permute-start | bytes 1105928 | tf_op jit(solution)/shard_map/ppermute | solution.py:181
  5.6 5.2 %collective-permute-start.1 = (bf16[720,256]{1,0:T(8,128)(2,1)}, bf16[720,256]{1,0:T(8,128)(2,1)S(1)}, u32[]{:S(2)}, u32[]{:S(2)}) collective-permute-start(bf16[720,256]{1,0:T(8,128)(2,1)} %bitcast.15), channel_id=1, source_target_pairs={{16,0},{32,16},{48,32},{64,48},{80,64},{96,80},{112,96},{128,112},... | collective-permute-start | bytes 1105928 | tf_op jit(solution)/shard_map/ppermute | solution.py:182
  10.8 0.0 collective-permute-done.below
  10.8 3.8 %collective-permute-done.1.above = bf16[720,256]{1,0:T(8,128)(2,1)S(1)} collective-permute-done((bf16[720,256]{1,0:T(8,128)(2,1)}, bf16[720,256]{1,0:T(8,128)(2,1)S(1)}, u32[]{:S(2)}, u32[]{:S(2)}) %collective-permute-start.1) | collective-permute-done | bytes 368672 | tf_op jit(solution)/shard_map/ppermute | solution.py:182
  14.6 0.6 copy-done.4
  15.3 0.0 copy-done.5
  15.3 0.0 copy-done.6
  15.3 1.0 %copy-done = bf16[4,256,256]{2,1,0:T(8,128)(2,1)S(1)} copy-done((bf16[4,256,256]{2,1,0:T(8,128)(2,1)S(1)}, bf16[4,256,256]{2,1,0:T(8,128)(2,1)}, u32[]{:S(2)}) %copy-start) | copy-done | bytes 524312
  16.4 1.0 %copy-done.2 = bf16[1,1,720,256]{3,2,1,0:T(8,128)(2,1)S(1)} copy-done((bf16[1,1,720,256]{3,2,1,0:T(8,128)(2,1)S(1)}, bf16[1,1,720,256]{3,2,1,0:T(8,128)(2,1)}, u32[]{:S(2)}) %copy-start.2) | copy-done | bytes 368664
  17.4 1.0 %copy-done.3 = bf16[1,1,720,256]{3,2,1,0:T(8,128)(2,1)S(1)} copy-done((bf16[1,1,720,256]{3,2,1,0:T(8,128)(2,1)S(1)}, bf16[1,1,720,256]{3,2,1,0:T(8,128)(2,1)}, u32[]{:S(2)}) %copy-start.3) | copy-done | bytes 368664
  18.3 5.4 %conv_forward.1 = (bf16[720,256]{1,0:T(8,128)(2,1)}, bf16[720,256]{1,0:T(8,128)(2,1)S(1)}, bf16[1024,256]{1,0:T(8,128)(2,1)S(1)}) custom-call(s32[1,16]{1,0:T(1,128)S(1)} %copy-done.4, s32[1,16]{1,0:T(1,128)S(1)} %copy-done.5, s32[1,16]{1,0:T(1,128)S(1)} %copy-done.6, f32[1,16]{1,0:T(1,128)S(1)} %convert_element_type.30.values, ...), custom_call_target="tpu_custom_call" | custom-call | flops 754974720 | bytes 16777216 | tf_op jit(solution)/shard_map/conv_forward/pallas_call | solution.py:122
  23.8 20.2 %all_to_all.15 = bf16[64,16,256]{2,1,0:T(8,128)(2,1)S(1)} all-to-all(bf16[64,16,256]{2,1,0:T(8,128)(2,1)S(1)} %bitcast.11), channel_id=1, replica_groups=mesh['za'=8,'zp'=2,'core'=2,'x'=4,'y'=4] {'zp','core','x','y'}, dimensions={0} | all-to-all | bytes 1048576 | tf_op jit(solution)/shard_map/all_to_all | solution.py:187
  44.0 0.1 reduce_sum.21
  44.1 26.2 %all_to_all.16 = bf16[8,16,256]{2,1,0:T(8,128)(2,1)S(1)} all-to-all(bf16[8,16,256]{2,1,0:T(8,128)(2,1)S(1)} %broadcast_in_dim.20), channel_id=1, replica_groups=mesh['za'=8,'zp'=2,'core'=2,'x'=4,'y'=4] {'za'}, dimensions={0} | all-to-all | bytes 131072 | tf_op jit(solution)/shard_map/all_to_all | solution.py:172
  70.3 0.8 broadcast_in_dim.21
  71.1 6.5 %all-to-all-start.2 = ((bf16[64,16,256]{2,1,0:T(8,128)(2,1)}), bf16[64,16,256]{2,1,0:T(8,128)(2,1)S(1)}, u32[]{:S(2)}, u32[]{:S(2)}) async-start(bf16[64,16,256]{2,1,0:T(8,128)(2,1)} %broadcast_in_dim.21), calls=%async_computation.2 | async-start | bytes 1048576 | tf_op jit(solution)/shard_map/all_to_all | solution.py:172
  77.6 3.1 %conv_backward.1 = (bf16[720,256]{1,0:T(8,128)(2,1)S(1)}, f32[720,256]{1,0:T(8,128)S(1)}, bf16[720,256]{1,0:T(8,128)(2,1)S(1)}) custom-call(s32[1,16]{1,0:T(1,128)S(1)} %copy-done.4, s32[1,16]{1,0:T(1,128)S(1)} %copy-done.5, s32[1,16]{1,0:T(1,128)S(1)} %copy-done.6, f32[1,16]{1,0:T(1,128)S(1)} %convert_element_type.30.values, ...), custom_call_target="tpu_custom_call" | custom-call | flops 377487360 | bytes 16777216 | tf_op jit(solution)/shard_map/conv_backward/pallas_call | solution.py:149
  80.7 3.7 %collective-permute-start.2 = (bf16[720,256]{1,0:T(8,128)(2,1)S(1)}, bf16[720,256]{1,0:T(8,128)(2,1)S(1)}, u32[]{:S(2)}, u32[]{:S(2)}) collective-permute-start(bf16[720,256]{1,0:T(8,128)(2,1)S(1)} %get-tuple-element.12), channel_id=1, source_target_pairs={{0,16},{16,32},{32,48},{48,64},{64,80},{80,96},{96,112},{112,128},... | collective-permute-start | bytes 1105928 | tf_op jit(solution)/shard_map/ppermute | solution.py:191
  84.4 1.9 %collective-permute-start.3 = (bf16[720,256]{1,0:T(8,128)(2,1)S(1)}, bf16[720,256]{1,0:T(8,128)(2,1)S(1)}, u32[]{:S(2)}, u32[]{:S(2)}) collective-permute-start(bf16[720,256]{1,0:T(8,128)(2,1)S(1)} %get-tuple-element.13), channel_id=1, source_target_pairs={{16,0},{32,16},{48,32},{64,48},{80,64},{96,80},{112,96},{128,112},... | collective-permute-start | bytes 1105928 | tf_op jit(solution)/shard_map/ppermute | solution.py:192
  86.4 2.5 %collective-permute-done.2 = bf16[720,256]{1,0:T(8,128)(2,1)S(1)} collective-permute-done((bf16[720,256]{1,0:T(8,128)(2,1)S(1)}, bf16[720,256]{1,0:T(8,128)(2,1)S(1)}, u32[]{:S(2)}, u32[]{:S(2)}) %collective-permute-start.2) | collective-permute-done | bytes 368672 | tf_op jit(solution)/shard_map/ppermute | solution.py:191
  88.9 4.4 %collective-permute-done.3 = bf16[720,256]{1,0:T(8,128)(2,1)S(1)} collective-permute-done((bf16[720,256]{1,0:T(8,128)(2,1)S(1)}, bf16[720,256]{1,0:T(8,128)(2,1)S(1)}, u32[]{:S(2)}, u32[]{:S(2)}) %collective-permute-start.3) | collective-permute-done | bytes 368672 | tf_op jit(solution)/shard_map/ppermute | solution.py:192
  93.3 0.9 fusion
  94.1 0.0 all-to-all-done.2
  94.1 1.1 %bitcast_convert_fusion = f32[4,256,256]{2,1,0:T(8,128)} fusion(bf16[4,256,256]{2,1,0:T(8,128)(2,1)S(1)} %bitcast.18), kind=kLoop, calls=%fused_computation.1 | loop fusion | flops 262144 | bytes 1572864 | tf_op jit(solution)/shard_map/convert_element_type | solution.py:198
  (14 shorter events, 0.0 us)
Async XLA Ops:
  0.6 10.1 %copy-start.7 = (bf16[1,16]{1,0:T(2,128)(2,1)S(1)}, bf16[1,16]{1,0:T(2,128)(2,1)}, u32[]{:S(2)}) copy-start(bf16[1,16]{1,0:T(2,128)(2,1)} %param.13) | copy-start | bytes 100
  0.6 10.1 %collective-permute-start = (bf16[720,256]{1,0:T(8,128)(2,1)}, bf16[720,256]{1,0:T(8,128)(2,1)S(1)}, u32[]{:S(2)}, u32[]{:S(2)}) collective-permute-start(bf16[720,256]{1,0:T(8,128)(2,1)} %bitcast.14), channel_id=1, source_target_pairs={{0,16},{16,32},{32,48},{48,64},{64,80},{80,96},{96,112},{112,128},... | collective-permute-start | bytes 1105928 | tf_op jit(solution)/shard_map/ppermute | solution.py:181
  5.6 9.0 %collective-permute-start.1 = (bf16[720,256]{1,0:T(8,128)(2,1)}, bf16[720,256]{1,0:T(8,128)(2,1)S(1)}, u32[]{:S(2)}, u32[]{:S(2)}) collective-permute-start(bf16[720,256]{1,0:T(8,128)(2,1)} %bitcast.15), channel_id=1, source_target_pairs={{16,0},{32,16},{48,32},{64,48},{80,64},{96,80},{112,96},{128,112},... | collective-permute-start | bytes 1105928 | tf_op jit(solution)/shard_map/ppermute | solution.py:182
  14.6 0.7 copy-start.4
  14.6 0.7 copy-start.5
  14.6 0.7 copy-start.6
  15.3 1.0 %copy-start = (bf16[4,256,256]{2,1,0:T(8,128)(2,1)S(1)}, bf16[4,256,256]{2,1,0:T(8,128)(2,1)}, u32[]{:S(2)}) copy-start(bf16[4,256,256]{2,1,0:T(8,128)(2,1)} %param.9) | copy-start | bytes 1572868
  16.4 1.0 %copy-start.2 = (bf16[1,1,720,256]{3,2,1,0:T(8,128)(2,1)S(1)}, bf16[1,1,720,256]{3,2,1,0:T(8,128)(2,1)}, u32[]{:S(2)}) copy-start(bf16[1,1,720,256]{3,2,1,0:T(8,128)(2,1)} %param.7) | copy-start | bytes 1105924
  17.3 1.0 %copy-start.3 = (bf16[1,1,720,256]{3,2,1,0:T(8,128)(2,1)S(1)}, bf16[1,1,720,256]{3,2,1,0:T(8,128)(2,1)}, u32[]{:S(2)}) copy-start(bf16[1,1,720,256]{3,2,1,0:T(8,128)(2,1)} %param.8) | copy-start | bytes 1105924
  71.1 6.5 %copy-start.1 = (bf16[4,256,256]{2,1,0:T(8,128)(2,1)S(1)}, bf16[4,256,256]{2,1,0:T(8,128)(2,1)}, u32[]{:S(2)}) copy-start(bf16[4,256,256]{2,1,0:T(8,128)(2,1)} %param.9) | copy-start | bytes 1572868
  71.1 23.0 %all-to-all-start.2 = ((bf16[64,16,256]{2,1,0:T(8,128)(2,1)}), bf16[64,16,256]{2,1,0:T(8,128)(2,1)S(1)}, u32[]{:S(2)}, u32[]{:S(2)}) async-start(bf16[64,16,256]{2,1,0:T(8,128)(2,1)} %broadcast_in_dim.21), calls=%async_computation.2 | async-start | bytes 1048576 | tf_op jit(solution)/shard_map/all_to_all | solution.py:172
  80.7 8.1 %collective-permute-start.2 = (bf16[720,256]{1,0:T(8,128)(2,1)S(1)}, bf16[720,256]{1,0:T(8,128)(2,1)S(1)}, u32[]{:S(2)}, u32[]{:S(2)}) collective-permute-start(bf16[720,256]{1,0:T(8,128)(2,1)S(1)} %get-tuple-element.12), channel_id=1, source_target_pairs={{0,16},{16,32},{32,48},{48,64},{64,80},{80,96},{96,112},{112,128},... | collective-permute-start | bytes 1105928 | tf_op jit(solution)/shard_map/ppermute | solution.py:191
  84.4 8.8 %collective-permute-start.3 = (bf16[720,256]{1,0:T(8,128)(2,1)S(1)}, bf16[720,256]{1,0:T(8,128)(2,1)S(1)}, u32[]{:S(2)}, u32[]{:S(2)}) collective-permute-start(bf16[720,256]{1,0:T(8,128)(2,1)S(1)} %get-tuple-element.13), channel_id=1, source_target_pairs={{16,0},{32,16},{48,32},{64,48},{80,64},{96,80},{112,96},{128,112},... | collective-permute-start | bytes 1105928 | tf_op jit(solution)/shard_map/ppermute | solution.py:192

commit v2 on v1

v2 whole, which is shorter than its diff:
```python
import functools
import math

import jax
import jax.numpy as jnp
import numpy as np
from jax import lax
from jax.experimental import pallas as pl
from jax.experimental.pallas import tpu as pltpu
from jax.sharding import Mesh
from jax.sharding import PartitionSpec as P

BF16 = jnp.bfloat16
F32 = jnp.float32
LANES = 128
SLAB = 48
VMEM_BYTES = 48 * 1024 * 1024
LAT = ("za", "zp", "core")
ENS = ("x", "y")
NEAR = ("zp", "core", "x", "y")
FAR = ("za",)


def pair_swap(axis, first):
    devices = range(lax.axis_size(axis))
    pairs = [(i, i + 1) for i in devices if i % 2 == first and i + 1 in devices]
    return pairs + [(j, i) for i, j in pairs]


def fill_twice(slabs, slot, field):
    lon_count = field.shape[0]
    for half in range(field.shape[1] // LANES):
        part = field[:, half * LANES : (half + 1) * LANES]
        slabs[slot + half, 0:lon_count, :] = part
        slabs[slot + half, lon_count : 2 * lon_count, :] = part


def near_kernel(sides, shifts, basis_ids, values, own, beside, summed, slabs):
    lon_count, channels = own.shape
    halves = channels // LANES
    fill_twice(slabs, 0, own[...].astype(F32))
    fill_twice(slabs, halves, beside[...].astype(F32))
    summed[...] = jnp.zeros_like(summed)

    def add_entry(entry, carry):
        source = (sides[0, entry] - 1) * halves
        target = basis_ids[0, entry] * halves
        shift = shifts[0, entry]
        value = values[0, entry]

        @pl.when(source >= 0)
        def _():
            for half in range(halves):
                summed[target + half] += value * slabs[source + half, pl.ds(shift, lon_count), :]

        return carry

    lax.fori_loop(0, sides.shape[1], add_entry, 0)


def mix_kernel(
    sides, shifts, basis_ids, values, distant, summed_in, weights_hbm, cotangent_hbm,
    activated_hbm, grad_pre, partial_w_hbm, summed,
    slabs, basis, preact, weights, cotangent, activated, partial_w, arrived, left,
):
    del summed_in
    lon_count, channels = distant.shape
    halves = channels // LANES
    basis_count = weights.shape[0] // channels
    get_weights = pltpu.make_async_copy(weights_hbm, weights, arrived.at[0])
    get_cotangent = pltpu.make_async_copy(cotangent_hbm, cotangent, arrived.at[1])
    get_weights.start()
    get_cotangent.start()
    fill_twice(slabs, 0, distant[...].astype(F32))

    def add_entry(entry, carry):
        target = basis_ids[0, entry] * halves
        shift = shifts[0, entry]
        value = values[0, entry]

        @pl.when(sides[0, entry] == 0)
        def _():
            for half in range(halves):
                summed[target + half] += value * slabs[half, pl.ds(shift, lon_count), :]

        return carry

    lax.fori_loop(0, sides.shape[1], add_entry, 0)
    for column in range(basis_count * halves):
        basis[:, column * LANES : (column + 1) * LANES] = summed[column].astype(BF16)
    get_weights.wait()
    preact[...] = jnp.dot(basis[...], weights[...], preferred_element_type=F32)
    get_cotangent.wait()

    def gelu_rows(step, carry):
        rows = pl.ds(pl.multiple_of(step * SLAB, SLAB), SLAB)
        v = preact[rows, :]
        root = math.sqrt(2.0 / math.pi)
        square = v * v
        bent = jnp.tanh(root * (v + 0.044715 * (v * square)))
        activated[rows, :] = (0.5 * v * (1.0 + bent)).astype(BF16)
        slope = 0.5 * (1.0 + bent) + 0.5 * v * (1.0 - bent * bent) * (
            root * (1.0 + (3.0 * 0.044715) * square)
        )
        grad_pre[rows, :] = (cotangent[rows, :].astype(F32) * slope).astype(BF16)
        return carry

    lax.fori_loop(0, lon_count // SLAB, gelu_rows, 0)
    put = [pltpu.make_async_copy(activated, activated_hbm, left.at[basis_count])]
    put[0].start()
    for k in range(basis_count):
        rows = slice(k * channels, (k + 1) * channels)
        partial_w[rows, :] = lax.dot_general(
            basis[:, rows], grad_pre[...], (((0,), (0,)), ((), ())), preferred_element_type=F32
        ).astype(BF16)
        put.append(
            pltpu.make_async_copy(partial_w.at[rows], partial_w_hbm.at[rows], left.at[k])
        )
        put[-1].start()
    for copy in put:
        copy.wait()


def backward_kernel(
    sides, shifts, basis_ids, values, grad_pre, weights, distant, own, beside, slabs, summed,
):
    lon_count, channels = grad_pre.shape
    halves = channels // LANES
    basis_count = weights.shape[0] // channels
    for k in range(basis_count):
        product = lax.dot_general(
            grad_pre[...],
            weights[k * channels : (k + 1) * channels, :],
            (((1,), (1,)), ((), ())),
            preferred_element_type=F32,
        )
        fill_twice(slabs, k * halves, product.astype(BF16).astype(F32))
    summed[...] = jnp.zeros_like(summed)

    def add_entry(entry, carry):
        target = sides[0, entry] * halves
        source = basis_ids[0, entry] * halves
        start = lon_count - shifts[0, entry]
        value = values[0, entry]
        for half in range(halves):
            summed[target + half] += value * slabs[source + half, pl.ds(start, lon_count), :]
        return carry

    lax.fori_loop(0, sides.shape[1], add_entry, 0)
    for slot, out in enumerate((distant, own, beside)):
        for half in range(halves):
            out[:, half * LANES : (half + 1) * LANES] = summed[slot * halves + half].astype(out.dtype)


def sum_kernel(scale, pieces, after, out):
    del after
    total = pieces[0].astype(F32)
    for i in range(1, pieces.shape[0]):
        total = total + pieces[i].astype(F32)
    total = (total * scale).astype(BF16)
    for i in range(out.shape[0]):
        out[i] = total


def specs(scalars, arrays, outside=0):
    return (
        [pl.BlockSpec(memory_space=pltpu.SMEM)] * scalars
        + [pl.BlockSpec(memory_space=pltpu.VMEM)] * arrays
        + [pl.BlockSpec(memory_space=pltpu.HBM)] * outside
    )


def params():
    return pltpu.CompilerParams(vmem_limit_bytes=VMEM_BYTES)


def shape(dims, dtype):
    return jax.ShapeDtypeStruct(dims, dtype)


def near_terms(tables, own, beside, wide):
    lon_count, channels = own.shape
    return pl.pallas_call(
        near_kernel,
        out_shape=shape((wide // LANES, lon_count, LANES), F32),
        in_specs=specs(4, 2),
        out_specs=specs(0, 1)[0],
        scratch_shapes=[pltpu.VMEM((2 * channels // LANES, 2 * lon_count, LANES), F32)],
        compiler_params=params(),
        cost_estimate=pl.CostEstimate(flops=0, bytes_accessed=8 << 20, transcendentals=0),
        name="near_terms",
    )(*tables, own, beside)


def mix(tables, distant, summed, weights, cotangent):
    lon_count, channels = distant.shape
    wide = weights.shape[0]
    return pl.pallas_call(
        mix_kernel,
        out_shape=(
            shape((lon_count, channels), BF16),
            shape((lon_count, channels), BF16),
            shape((wide, channels), BF16),
            shape(summed.shape, F32),
        ),
        in_specs=specs(4, 2, 2),
        out_specs=tuple(specs(0, 0, 1) + specs(0, 1) + specs(0, 0, 1) + specs(0, 1)),
        input_output_aliases={5: 3},
        scratch_shapes=[
            pltpu.VMEM((channels // LANES, 2 * lon_count, LANES), F32),
            pltpu.VMEM((lon_count, wide), BF16),
            pltpu.VMEM((lon_count, channels), F32),
            pltpu.VMEM((wide, channels), BF16),
            pltpu.VMEM((lon_count, channels), BF16),
            pltpu.VMEM((lon_count, channels), BF16),
            pltpu.VMEM((wide, channels), BF16),
            pltpu.SemaphoreType.DMA((2,)),
            pltpu.SemaphoreType.DMA((wide // channels + 1,)),
        ],
        compiler_params=params(),
        cost_estimate=pl.CostEstimate(
            flops=4 * lon_count * wide * channels, bytes_accessed=8 << 20, transcendentals=0
        ),
        name="mix",
    )(*tables, distant, summed, weights, cotangent)[:3]


def backward(tables, grad_pre, weights):
    lon_count, channels = grad_pre.shape
    halves = channels // LANES
    wide = weights.shape[0]
    return pl.pallas_call(
        backward_kernel,
        out_shape=(
            shape((lon_count, channels), BF16),
            shape((lon_count, channels), F32),
            shape((lon_count, channels), BF16),
        ),
        in_specs=specs(4, 2),
        out_specs=tuple(specs(0, 3)),
        scratch_shapes=[
            pltpu.VMEM((wide // LANES, 2 * lon_count, LANES), F32),
            pltpu.VMEM((3 * halves, lon_count, LANES), F32),
        ],
        compiler_params=params(),
        cost_estimate=pl.CostEstimate(
            flops=2 * lon_count * wide * channels, bytes_accessed=8 << 20, transcendentals=0
        ),
        name="backward",
    )(*tables, grad_pre, weights)


def summed_copies(pieces, count, scale, after):
    return pl.pallas_call(
        functools.partial(sum_kernel, scale),
        out_shape=shape((count,) + pieces.shape[1:], BF16),
        in_specs=specs(0, 1) + [pl.BlockSpec(memory_space=pl.ANY)],
        out_specs=specs(0, 1)[0],
        compiler_params=params(),
        name="summed_copies",
    )(pieces, after)


def on_device(inputs, cotangent, weights, cycle_offsets, lon_shifts, basis_ids, entry_values):
    own = inputs[0, 0]
    lon_count, channels = own.shape
    basis_count = weights.shape[0]
    wide = basis_count * channels
    flat_weights = weights.reshape(wide, channels)
    off_chip, on_chip = pair_swap(LAT, 1), pair_swap(LAT, 0)
    sides = 1 + cycle_offsets * (1 - 2 * lax.axis_index("core"))
    tables = (sides, lon_shifts, basis_ids, entry_values.astype(F32))
    distant = lax.ppermute(own, LAT, off_chip)
    beside = lax.ppermute(own, LAT, on_chip)
    summed = near_terms(tables, own, beside, wide)
    activated, grad_pre, partial_w = mix(tables, distant, summed, flat_weights, cotangent[0, 0])

    near, far = lax.axis_size(NEAR), lax.axis_size(FAR)
    pieces = lax.all_to_all(partial_w.reshape(near, -1, channels), NEAR, 0, 0)
    to_distant, middle, to_beside = backward(tables, grad_pre, flat_weights)
    from_distant = lax.ppermute(to_distant, LAT, off_chip)
    from_beside = lax.ppermute(to_beside, LAT, on_chip)
    field_gradient = (middle + from_distant.astype(F32) + from_beside.astype(F32)).astype(BF16)

    cell_count = lax.axis_size(LAT) * lax.axis_size(ENS) * lon_count
    copies = summed_copies(pieces, far, 1.0, to_beside)
    pieces = lax.all_to_all(copies, FAR, 0, 0)
    copies = summed_copies(pieces, near, 1.0 / math.sqrt(cell_count), field_gradient)
    whole = lax.all_to_all(copies, NEAR, 0, 0)
    grad_weights = whole.reshape(basis_count, channels, channels).astype(F32)
    return (activated[None, None], field_gradient[None, None], grad_weights)


def solution(mesh):
    lat_count, ens_count = mesh.devices.shape
    grid = Mesh(
        np.asarray(mesh.devices).reshape(lat_count // 4, 2, 2, 4, ens_count // 4),
        LAT + ENS,
    )
    placed = (
        P(ENS, LAT, None, None),
        P(ENS, LAT, None, None),
        P(),
        P(LAT, None),
        P(LAT, None),
        P(LAT, None),
        P(LAT, None),
    )
    return jax.shard_map(
        on_device,
        mesh=grid,
        in_specs=placed,
        out_specs=(P(ENS, LAT, None, None), P(ENS, LAT, None, None), P()),
        check_vma=False,
    )
```

time: 95.7 us -> 86.8 us (0.907)
  blocking collectives: 46.4 us -> 18.1 us
  starting transfers between devices: 22.2 us -> 34 us
  waiting for transfers between devices: 10.7 us -> 17.2 us
  Pallas kernels: 8.55 us -> 11.5 us
  local copies, waits for them, and re-layouts: 4.54 us -> 2.32 us
    all_to_all x2 -> x1, blocking collectives: 46.4 us -> 18.1 us  [on_device(): whole = lax.all_to_all(copies, NEAR, 0, 0)]
    all_to_all x1 -> x2, waiting for transfers between devices: 0.01 us -> 15.6 us  [the longest x1 12.8 us: on_device(): pieces = lax.all_to_all(copies, FAR, 0, 0)]
    all_to_all x1 -> x2, starting transfers between devices: 6.47 us -> 18.3 us  [the longest x1 14.1 us: on_device(): pieces = lax.all_to_all(copies, FAR, 0, 0)]
    ppermute x4, waiting for transfers between devices: 10.7 us -> 1.58 us  [the longest x1 1.58 us: on_device(): distant = lax.ppermute(own, LAT, off_chip)]
    pallas_call x2 -> x5, Pallas kernels: 8.55 us -> 11.5 us  [the longest x1 5.63 us: mix(): pl.pallas_call(mix_kernel, out_shape=(shape((lon_count, channels), BF16),...]
    unnamed x16, local copies, waits for them, and re-layouts: 3.71 us -> 2.32 us
  transfers between devices with their start and end apart: 5 -> 6, of which waited for: 3 -> 3; matrix products, arithmetic and copies ran while one was open for 1% -> 2% of each run, Pallas kernels for 3% -> 7%
where the time goes in v2:
time: 86.8 us; the launch traced here: 86.3 us
  starting transfers between devices  34 us (39%)
  blocking collectives  18.1 us (21%)
  waiting for transfers between devices  17.2 us (20%)
  Pallas kernels  11.5 us (13%)
  other arithmetic  2.49 us (3%)
  local copies, waits for them, and re-layouts  2.32 us (3%)
    all_to_all x1, blocking collectives, on_device(): whole = lax.all_to_all(copies, NEAR, 0, 0)  18.1 us
    all_to_all x1, starting transfers between devices, on_device(): pieces = lax.all_to_all(copies, FAR, 0, 0)  14.1 us
    all_to_all x1, waiting for transfers between devices, on_device(): pieces = lax.all_to_all(copies, FAR, 0, 0)  12.8 us
    ppermute x1, starting transfers between devices, on_device(): beside = lax.ppermute(own, LAT, on_chip)  8.92 us
    pallas_call x1, Pallas kernels, mix(): pl.pallas_call(mix_kernel, out_shape=(shape((lon_count, channels), BF16),...  5.63 us
    all_to_all x1, starting transfers between devices, on_device(): pieces = lax.all_to_all(partial_w.reshape(near, -1, channels), NEAR, 0, 0)  4.21 us
    pallas_call x1, Pallas kernels, backward(): pl.pallas_call(backward_kernel, out_shape=(shape((lon_count, channels), B...  3.19 us
    ppermute x1, starting transfers between devices, on_device(): from_distant = lax.ppermute(to_distant, LAT, off_chip)  2.91 us
  transfers between devices with their start and end apart: 6, of which 3 were waited for; matrix products, arithmetic and copies ran while one was open for 2% of the time, Pallas kernels for 7%

profile of v2, /device:TPU:1, one launch (start us, length us, event | category | flops | bytes accessed | tf_op | source)
XLA Modules:
  0.0 86.3 jit_solution(1549169837462024366)
XLA Ops:
  0.6 8.9 %collective-permute-start.1 = (bf16[720,256]{1,0:T(8,128)(2,1)}, bf16[720,256]{1,0:T(8,128)(2,1)S(1)}, u32[]{:S(2)}, u32[]{:S(2)}) collective-permute-start(bf16[720,256]{1,0:T(8,128)(2,1)} %bitcast.13), channel_id=1, source_target_pairs={{0,16},{32,48},{64,80},{96,112},{128,144},{160,176},{192,208},{224... | collective-permute-start | bytes 1105928 | tf_op jit(solution)/shard_map/ppermute | solution.py:274
  9.6 1.9 %collective-permute-start = (bf16[720,256]{1,0:T(8,128)(2,1)}, bf16[720,256]{1,0:T(8,128)(2,1)S(1)}, u32[]{:S(2)}, u32[]{:S(2)}) collective-permute-start(bf16[720,256]{1,0:T(8,128)(2,1)} %bitcast.14), channel_id=1, source_target_pairs={{16,32},{48,64},{80,96},{112,128},{144,160},{176,192},{208,224},{2... | collective-permute-start | bytes 1105928 | tf_op jit(solution)/shard_map/ppermute | solution.py:273
  11.5 0.7 convert_element_type.18.values
  12.2 0.7 multiply_add_fusion.sides
  12.8 1.0 %copy-done.2 = bf16[1,1,720,256]{3,2,1,0:T(8,128)(2,1)S(1)} copy-done((bf16[1,1,720,256]{3,2,1,0:T(8,128)(2,1)S(1)}, bf16[1,1,720,256]{3,2,1,0:T(8,128)(2,1)}, u32[]{:S(2)}) %copy-start.2) | copy-done | bytes 368664
  13.8 0.7 copy-done.4
  14.5 0.7 copy-done.6
  15.1 1.9 %near_terms.1.summed_in = f32[8,720,128]{2,1,0:T(8,128)S(1)} custom-call(s32[1,16]{1,0:T(1,128)S(1)} %multiply_add_fusion.sides, s32[1,16]{1,0:T(1,128)S(1)} %copy-done.4, s32[1,16]{1,0:T(1,128)S(1)} %copy-done.6, f32[1,16]{1,0:T(1,128)S(1)} %convert_element_type.18.values, bf16[720,256]{1,0:T(8,128)(2,1)S(1)} %bitcast.15, ...), custom_call_target="tpu_custom_call" | custom-call | bytes 8388608 | tf_op jit(solution)/shard_map/near_terms/pallas_call | solution.py:183
  17.0 0.0 copy-start.5
  17.0 0.0 copy-start.7
  17.0 1.6 %collective-permute-done.distant = bf16[720,256]{1,0:T(8,128)(2,1)S(1)} collective-permute-done((bf16[720,256]{1,0:T(8,128)(2,1)}, bf16[720,256]{1,0:T(8,128)(2,1)S(1)}, u32[]{:S(2)}, u32[]{:S(2)}) %collective-permute-start) | collective-permute-done | bytes 368672 | tf_op jit(solution)/shard_map/ppermute | solution.py:273
  18.6 5.6 %mix.1 = (bf16[720,256]{1,0:T(8,128)(2,1)}, bf16[720,256]{1,0:T(8,128)(2,1)S(1)}, bf16[1024,256]{1,0:T(8,128)(2,1)}, f32[8,720,128]{2,1,0:T(8,128)S(1)}) custom-call(s32[1,16]{1,0:T(1,128)S(1)} %multiply_add_fusion.sides, s32[1,16]{1,0:T(1,128)S(1)} %copy-done.4, s32[1,16]{1,0:T(1,128)S(1)} %copy-done.6, ...), custom_call_target="tpu_custom_call", output_to_operand_aliasing={{3}: (5, {})} | custom-call | flops 754974720 | bytes 8388608 | tf_op jit(solution)/shard_map/mix/pallas_call | solution.py:198
  24.3 4.2 %all-to-all-start = ((bf16[64,16,256]{2,1,0:T(8,128)(2,1)}), bf16[64,16,256]{2,1,0:T(8,128)(2,1)S(1)}, u32[]{:S(2)}, u32[]{:S(2)}) async-start(bf16[64,16,256]{2,1,0:T(8,128)(2,1)} %bitcast.5), calls=%async_computation | async-start | bytes 1048576 | tf_op jit(solution)/shard_map/all_to_all | solution.py:279
  28.5 3.2 %backward.1 = (bf16[720,256]{1,0:T(8,128)(2,1)S(1)}, f32[720,256]{1,0:T(8,128)S(1)}, bf16[720,256]{1,0:T(8,128)(2,1)S(1)}) custom-call(s32[1,16]{1,0:T(1,128)S(1)} %multiply_add_fusion.sides, s32[1,16]{1,0:T(1,128)S(1)} %copy-done.5, s32[1,16]{1,0:T(1,128)S(1)} %copy-done.7, f32[1,16]{1,0:T(1,128)S(1)} %convert_element_type.18.values, ...), custom_call_target="tpu_custom_call" | custom-call | flops 377487360 | bytes 8388608 | tf_op jit(solution)/shard_map/backward/pallas_call | solution.py:232
  31.7 2.9 %collective-permute-start.2 = (bf16[720,256]{1,0:T(8,128)(2,1)S(1)}, bf16[720,256]{1,0:T(8,128)(2,1)S(1)}, u32[]{:S(2)}, u32[]{:S(2)}) collective-permute-start(bf16[720,256]{1,0:T(8,128)(2,1)S(1)} %get-tuple-element.12), channel_id=1, source_target_pairs={{16,32},{48,64},{80,96},{112,128},{144,160},{176,192},{208,224},{2... | collective-permute-start | bytes 1105928 | tf_op jit(solution)/shard_map/ppermute | solution.py:281
  34.6 1.9 %collective-permute-start.3 = (bf16[720,256]{1,0:T(8,128)(2,1)S(1)}, bf16[720,256]{1,0:T(8,128)(2,1)S(1)}, u32[]{:S(2)}, u32[]{:S(2)}) collective-permute-start(bf16[720,256]{1,0:T(8,128)(2,1)S(1)} %get-tuple-element.13.after), channel_id=1, source_target_pairs={{0,16},{32,48},{64,80},{96,112},{128,144},{160,176},{192,208},{224... | collective-permute-start | bytes 1105928 | tf_op jit(solution)/shard_map/ppermute | solution.py:282
  36.5 2.9 %all-to-all-done.pieces = bf16[64,16,256]{2,1,0:T(8,128)(2,1)S(1)} async-done(((bf16[64,16,256]{2,1,0:T(8,128)(2,1)}), bf16[64,16,256]{2,1,0:T(8,128)(2,1)S(1)}, u32[]{:S(2)}, u32[]{:S(2)}) %all-to-all-start) | async-done | bytes 524320 | tf_op jit(solution)/shard_map/all_to_all | solution.py:279
  39.4 0.7 summed_copies.2
  40.1 14.1 %all-to-all-start.1 = ((bf16[8,16,256]{2,1,0:T(8,128)(2,1)}), bf16[8,16,256]{2,1,0:T(8,128)(2,1)S(1)}, u32[]{:S(2)}, u32[]{:S(2)}) async-start(bf16[8,16,256]{2,1,0:T(8,128)(2,1)} %summed_copies.2), calls=%async_computation.1 | async-start | bytes 131072 | tf_op jit(solution)/shard_map/all_to_all | solution.py:287
  54.2 0.1 add_convert_fusion.after
  54.3 0.0 copy-start
  54.4 12.8 %all-to-all-done.1.pieces = bf16[8,16,256]{2,1,0:T(8,128)(2,1)S(1)} async-done(((bf16[8,16,256]{2,1,0:T(8,128)(2,1)}), bf16[8,16,256]{2,1,0:T(8,128)(2,1)S(1)}, u32[]{:S(2)}, u32[]{:S(2)}) %all-to-all-start.1) | async-done | bytes 65568 | tf_op jit(solution)/shard_map/all_to_all | solution.py:287
  67.2 18.1 %all_to_all.15 = bf16[64,16,256]{2,1,0:T(8,128)(2,1)S(1)} all-to-all(bf16[64,16,256]{2,1,0:T(8,128)(2,1)S(1)} %summed_copies.3), channel_id=1, replica_groups=mesh['za'=8,'zp'=2,'core'=2,'x'=4,'y'=4] {'zp','core','x','y'}, dimensions={0} | all-to-all | bytes 1048576 | tf_op jit(solution)/shard_map/all_to_all | solution.py:289
  85.3 1.1 %bitcast_convert_fusion = f32[4,256,256]{2,1,0:T(8,128)} fusion(bf16[4,256,256]{2,1,0:T(8,128)(2,1)S(1)} %bitcast.17), kind=kLoop, calls=%fused_computation.1 | loop fusion | flops 262144 | bytes 1572864 | tf_op jit(solution)/shard_map/convert_element_type | solution.py:290
  (14 shorter events, 0.1 us)
Async XLA Ops:
  0.6 18.0 %copy-start.1 = (bf16[4,256,256]{2,1,0:T(8,128)(2,1)S(1)}, bf16[4,256,256]{2,1,0:T(8,128)(2,1)}, u32[]{:S(2)}) copy-start(bf16[4,256,256]{2,1,0:T(8,128)(2,1)} %param.9) | copy-start | bytes 1572868
  0.6 12.2 %collective-permute-start.1 = (bf16[720,256]{1,0:T(8,128)(2,1)}, bf16[720,256]{1,0:T(8,128)(2,1)S(1)}, u32[]{:S(2)}, u32[]{:S(2)}) collective-permute-start(bf16[720,256]{1,0:T(8,128)(2,1)} %bitcast.13), channel_id=1, source_target_pairs={{0,16},{32,48},{64,80},{96,112},{128,144},{160,176},{192,208},{224... | collective-permute-start | bytes 1105928 | tf_op jit(solution)/shard_map/ppermute | solution.py:274
  9.6 9.0 %collective-permute-start = (bf16[720,256]{1,0:T(8,128)(2,1)}, bf16[720,256]{1,0:T(8,128)(2,1)S(1)}, u32[]{:S(2)}, u32[]{:S(2)}) collective-permute-start(bf16[720,256]{1,0:T(8,128)(2,1)} %bitcast.14), channel_id=1, source_target_pairs={{16,32},{48,64},{80,96},{112,128},{144,160},{176,192},{208,224},{2... | collective-permute-start | bytes 1105928 | tf_op jit(solution)/shard_map/ppermute | solution.py:273
  12.8 1.0 %copy-start.2 = (bf16[1,1,720,256]{3,2,1,0:T(8,128)(2,1)S(1)}, bf16[1,1,720,256]{3,2,1,0:T(8,128)(2,1)}, u32[]{:S(2)}) copy-start(bf16[1,1,720,256]{3,2,1,0:T(8,128)(2,1)} %param.7) | copy-start | bytes 1105924
  13.8 0.7 copy-start.4
  14.5 0.7 copy-start.6
  15.1 3.5 %copy-start.3 = (bf16[1,1,720,256]{3,2,1,0:T(8,128)(2,1)S(1)}, bf16[1,1,720,256]{3,2,1,0:T(8,128)(2,1)}, u32[]{:S(2)}) copy-start(bf16[1,1,720,256]{3,2,1,0:T(8,128)(2,1)} %param.8) | copy-start | bytes 1105924
  17.0 11.5 %copy-start.5 = (s32[1,16]{1,0:T(1,128)S(1)}, s32[1,16]{1,0:T(1,128)}, u32[]{:S(2)}) copy-start(s32[1,16]{1,0:T(1,128)} %shifts.5) | copy-start | bytes 196
  17.0 11.5 %copy-start.7 = (s32[1,16]{1,0:T(1,128)S(1)}, s32[1,16]{1,0:T(1,128)}, u32[]{:S(2)}) copy-start(s32[1,16]{1,0:T(1,128)} %basis_ids.5) | copy-start | bytes 196
  24.3 15.1 %all-to-all-start = ((bf16[64,16,256]{2,1,0:T(8,128)(2,1)}), bf16[64,16,256]{2,1,0:T(8,128)(2,1)S(1)}, u32[]{:S(2)}, u32[]{:S(2)}) async-start(bf16[64,16,256]{2,1,0:T(8,128)(2,1)} %bitcast.5), calls=%async_computation | async-start | bytes 1048576 | tf_op jit(solution)/shard_map/all_to_all | solution.py:279
  31.7 22.5 %collective-permute-start.2 = (bf16[720,256]{1,0:T(8,128)(2,1)S(1)}, bf16[720,256]{1,0:T(8,128)(2,1)S(1)}, u32[]{:S(2)}, u32[]{:S(2)}) collective-permute-start(bf16[720,256]{1,0:T(8,128)(2,1)S(1)} %get-tuple-element.12), channel_id=1, source_target_pairs={{16,32},{48,64},{80,96},{112,128},{144,160},{176,192},{208,224},{2... | collective-permute-start | bytes 1105928 | tf_op jit(solution)/shard_map/ppermute | solution.py:281
  34.6 19.6 %collective-permute-start.3 = (bf16[720,256]{1,0:T(8,128)(2,1)S(1)}, bf16[720,256]{1,0:T(8,128)(2,1)S(1)}, u32[]{:S(2)}, u32[]{:S(2)}) collective-permute-start(bf16[720,256]{1,0:T(8,128)(2,1)S(1)} %get-tuple-element.13.after), channel_id=1, source_target_pairs={{0,16},{32,48},{64,80},{96,112},{128,144},{160,176},{192,208},{224... | collective-permute-start | bytes 1105928 | tf_op jit(solution)/shard_map/ppermute | solution.py:282
  40.1 27.0 %all-to-all-start.1 = ((bf16[8,16,256]{2,1,0:T(8,128)(2,1)}), bf16[8,16,256]{2,1,0:T(8,128)(2,1)S(1)}, u32[]{:S(2)}, u32[]{:S(2)}) async-start(bf16[8,16,256]{2,1,0:T(8,128)(2,1)} %summed_copies.2), calls=%async_computation.1 | async-start | bytes 131072 | tf_op jit(solution)/shard_map/all_to_all | solution.py:287
  54.3 32.0 %copy-start = (bf16[720,256]{1,0:T(8,128)(2,1)}, bf16[720,256]{1,0:T(8,128)(2,1)S(1)}, u32[]{:S(2)}) copy-start(bf16[720,256]{1,0:T(8,128)(2,1)S(1)} %add_convert_fusion.after) | copy-start | bytes 1105924

commit v3 on v2

v3 whole, which is shorter than its diff:
```python
import math

import jax
import jax.numpy as jnp
import numpy as np
from jax import lax
from jax.experimental import pallas as pl
from jax.experimental.pallas import tpu as pltpu
from jax.sharding import Mesh
from jax.sharding import PartitionSpec as P

BF16 = jnp.bfloat16
F32 = jnp.float32
LANES = 128
SLAB = 48
PARTS = 3
VMEM_BYTES = 48 * 1024 * 1024
LAT = ("za", "zp", "core")
ENS = ("x", "y")
NEAR = ("zp", "core", "x", "y")
FAR = ("za",)


def pair_swap(axis, first):
    devices = range(lax.axis_size(axis))
    pairs = [(i, i + 1) for i in devices if i % 2 == first and i + 1 in devices]
    return pairs + [(j, i) for i, j in pairs]


def fill_twice(slabs, slot, field):
    lon_count = field.shape[0]
    for half in range(field.shape[1] // LANES):
        part = field[:, half * LANES : (half + 1) * LANES]
        slabs[slot + half, 0:lon_count, :] = part
        slabs[slot + half, lon_count : 2 * lon_count, :] = part


def fetched(tables, held, arrived):
    copies = [pltpu.make_async_copy(t, h, arrived.at[i]) for i, (t, h) in enumerate(zip(tables, held))]
    for copy in copies:
        copy.start()
    return copies


def spread(values, rows):
    count = values.shape[1]
    wide = jnp.broadcast_to(values[...].astype(F32), (count, count))
    row = lax.broadcasted_iota(jnp.int32, (count, count), 0)
    column = lax.broadcasted_iota(jnp.int32, (count, count), 1)
    picked = jnp.sum(jnp.where(row == column, wide, 0.0), axis=1, keepdims=True)
    rows[...] = jnp.broadcast_to(picked, rows.shape)


def add_rows(total, source, value, halves, target, slot, start):
    lon_count = total.shape[1]
    for half in range(halves):
        total[target + half] += value * source[slot + half, pl.ds(start, lon_count), :]


def own_kernel(
    offsets_hbm, shifts_hbm, basis_ids_hbm, values, own_hbm, summed, coefs,
    offsets, shifts, basis_ids, own, slabs, arrived,
):
    halves = own.shape[1] // LANES
    copies = fetched(
        (offsets_hbm, shifts_hbm, basis_ids_hbm, own_hbm), (offsets, shifts, basis_ids, own), arrived
    )
    spread(values, coefs)
    summed[...] = jnp.zeros_like(summed)
    for copy in copies:
        copy.wait()
    fill_twice(slabs, 0, own[...].astype(F32))

    def add_entry(entry, carry):
        @pl.when(offsets[0, entry] == 0)
        def _():
            add_rows(
                summed, slabs, coefs[pl.ds(entry, 1), :], halves,
                basis_ids[0, entry] * halves, 0, shifts[0, entry],
            )

        return carry

    lax.fori_loop(0, offsets.shape[1], add_entry, 0)


def mix_kernel(
    offsets_hbm, shifts_hbm, basis_ids_hbm, coefs, beside, distant, summed_in, weights_hbm, cotangent_hbm,
    activated_hbm, grad_pre, partial_w_hbm, summed,
    offsets, shifts, basis_ids, slabs, basis, weights, cotangent, activated, partial_w,
    arrived, left,
):
    del summed_in
    lon_count, channels = distant.shape
    halves = channels // LANES
    basis_count = weights.shape[0] // channels
    copies = fetched(
        (offsets_hbm, shifts_hbm, basis_ids_hbm, weights_hbm, cotangent_hbm),
        (offsets, shifts, basis_ids, weights, cotangent),
        arrived,
    )
    for copy in copies[:3]:
        copy.wait()
    fill_twice(slabs, 0, distant[...].astype(F32))
    fill_twice(slabs, halves, beside[...].astype(F32))
    turn = 1 - 2 * lax.axis_index("core")

    def add_entry(entry, carry):
        side = offsets[0, entry] * turn

        @pl.when(side != 0)
        def _():
            add_rows(
                summed, slabs, coefs[pl.ds(entry, 1), :], halves,
                basis_ids[0, entry] * halves, (side + 1) // 2 * halves, shifts[0, entry],
            )

        return carry

    lax.fori_loop(0, offsets.shape[1], add_entry, 0)
    copies[3].wait()
    copies[4].wait()
    root = math.sqrt(2.0 / math.pi)
    part = lon_count // PARTS
    for first in range(0, lon_count, part):
        rows = slice(first, first + part)
        for column in range(basis_count * halves):
            basis[rows, column * LANES : (column + 1) * LANES] = summed[column, rows, :].astype(BF16)
        preact = jnp.dot(basis[rows, :], weights[...], preferred_element_type=F32)
        for slab in range(0, part, SLAB):
            v = preact[slab : slab + SLAB]
            inner = slice(first + slab, first + slab + SLAB)
            square = v * v
            bent = jnp.tanh(v * (root + (root * 0.044715) * square))
            half_sum = 0.5 + 0.5 * bent
            activated[inner, :] = (v * half_sum).astype(BF16)
            slope = half_sum + (v * (0.5 - 0.5 * (bent * bent))) * (
                root + (3.0 * 0.044715 * root) * square
            )
            grad_pre[inner, :] = (cotangent[inner, :].astype(F32) * slope).astype(BF16)
    put = [pltpu.make_async_copy(activated, activated_hbm, left.at[basis_count])]
    put[0].start()
    for k in range(basis_count):
        rows = slice(k * channels, (k + 1) * channels)
        partial_w[rows, :] = lax.dot_general(
            basis[:, rows], grad_pre[...], (((0,), (0,)), ((), ())), preferred_element_type=F32
        ).astype(BF16)
        put.append(
            pltpu.make_async_copy(partial_w.at[rows], partial_w_hbm.at[rows], left.at[k])
        )
        put[-1].start()
    for copy in put:
        copy.wait()


def backward_kernel(
    offsets_hbm, shifts_hbm, basis_ids_hbm, coefs, grad_pre, weights_hbm, distant, own, beside,
    offsets, shifts, basis_ids, weights, slabs, summed, arrived,
):
    lon_count, channels = grad_pre.shape
    halves = channels // LANES
    basis_count = weights.shape[0] // channels
    copies = fetched(
        (offsets_hbm, shifts_hbm, basis_ids_hbm, weights_hbm),
        (offsets, shifts, basis_ids, weights),
        arrived,
    )
    summed[...] = jnp.zeros_like(summed)
    for copy in copies:
        copy.wait()
    for k in range(basis_count):
        product = lax.dot_general(
            grad_pre[...],
            weights[k * channels : (k + 1) * channels, :],
            (((1,), (1,)), ((), ())),
            preferred_element_type=F32,
        )
        fill_twice(slabs, k * halves, product.astype(BF16).astype(F32))
    turn = 1 - 2 * lax.axis_index("core")

    def add_entry(entry, carry):
        add_rows(
            summed, slabs, coefs[pl.ds(entry, 1), :], halves,
            (offsets[0, entry] * turn + 1) * halves, basis_ids[0, entry] * halves,
            lon_count - shifts[0, entry],
        )
        return carry

    lax.fori_loop(0, offsets.shape[1], add_entry, 0)
    for slot, out in enumerate((distant, own, beside)):
        for half in range(halves):
            out[:, half * LANES : (half + 1) * LANES] = summed[slot * halves + half].astype(out.dtype)


def vmem():
    return pl.BlockSpec(memory_space=pltpu.VMEM)


def hbm():
    return pl.BlockSpec(memory_space=pltpu.HBM)


def kept_out(arrays):
    return [pltpu.with_memory_space_constraint(array, pltpu.HBM) for array in arrays]


def params():
    return pltpu.CompilerParams(vmem_limit_bytes=VMEM_BYTES)


def cost(flops, mib):
    return pl.CostEstimate(flops=flops, bytes_accessed=mib << 20, transcendentals=0)


def shape(dims, dtype):
    return jax.ShapeDtypeStruct(dims, dtype)


def table_scratch(entry_count):
    return [pltpu.SMEM((1, entry_count), jnp.int32)] * 3


def own_terms(tables, values, own, wide):
    lon_count, channels = own.shape
    entry_count = values.shape[1]
    return pl.pallas_call(
        own_kernel,
        out_shape=(
            shape((wide // LANES, lon_count, LANES), F32),
            shape((entry_count, LANES), F32),
        ),
        in_specs=[hbm()] * 3 + [vmem(), hbm()],
        out_specs=(vmem(), vmem()),
        scratch_shapes=table_scratch(entry_count)
        + [
            pltpu.VMEM((lon_count, channels), BF16),
            pltpu.VMEM((channels // LANES, 2 * lon_count, LANES), F32),
            pltpu.SemaphoreType.DMA((4,)),
        ],
        compiler_params=params(),
        cost_estimate=cost(0, 4),
        name="own_terms",
    )(*kept_out(tables), values, *kept_out([own]))


def mix(tables, coefs, distant, beside, summed, weights, cotangent):
    lon_count, channels = distant.shape
    wide = weights.shape[0]
    field = pltpu.VMEM((lon_count, channels), BF16)
    square = pltpu.VMEM((wide, channels), BF16)
    return pl.pallas_call(
        mix_kernel,
        out_shape=(
            shape((lon_count, channels), BF16),
            shape((lon_count, channels), BF16),
            shape((wide, channels), BF16),
            shape(summed.shape, F32),
        ),
        in_specs=[hbm()] * 3 + [vmem()] * 4 + [hbm()] * 2,
        out_specs=(hbm(), vmem(), hbm(), vmem()),
        input_output_aliases={6: 3},
        scratch_shapes=table_scratch(coefs.shape[0])
        + [
            pltpu.VMEM((2 * channels // LANES, 2 * lon_count, LANES), F32),
            pltpu.VMEM((lon_count, wide), BF16),
            square,
            field,
            field,
            square,
            pltpu.SemaphoreType.DMA((5,)),
            pltpu.SemaphoreType.DMA((wide // channels + 1,)),
        ],
        compiler_params=params(),
        cost_estimate=cost(4 * lon_count * wide * channels, 8),
        name="mix",
    )(*kept_out(tables), coefs, beside, distant, summed, *kept_out([weights, cotangent]))[:3]


def backward(tables, coefs, grad_pre, weights):
    lon_count, channels = grad_pre.shape
    halves = channels // LANES
    wide = weights.shape[0]
    return pl.pallas_call(
        backward_kernel,
        out_shape=(
            shape((lon_count, channels), BF16),
            shape((lon_count, channels), F32),
            shape((lon_count, channels), BF16),
        ),
        in_specs=[hbm()] * 3 + [vmem()] * 2 + [hbm()],
        out_specs=(vmem(), vmem(), vmem()),
        scratch_shapes=table_scratch(coefs.shape[0])
        + [
            pltpu.VMEM((wide, channels), BF16),
            pltpu.VMEM((wide // LANES, 2 * lon_count, LANES), F32),
            pltpu.VMEM((3 * halves, lon_count, LANES), F32),
            pltpu.SemaphoreType.DMA((4,)),
        ],
        compiler_params=params(),
        cost_estimate=cost(2 * lon_count * wide * channels, 8),
        name="backward",
    )(*kept_out(tables), coefs, grad_pre, *kept_out([weights]))


def to_all(block, axes):
    count = lax.axis_size(axes)
    return lax.all_to_all(jnp.broadcast_to(block[None], (count,) + block.shape), axes, 0, 0)


def on_device(inputs, cotangent, weights, cycle_offsets, lon_shifts, basis_ids, entry_values):
    own = inputs[0, 0]
    lon_count, channels = own.shape
    basis_count = weights.shape[0]
    wide = basis_count * channels
    flat_weights = weights.reshape(wide, channels)
    off_chip, on_chip = pair_swap(LAT, 1), pair_swap(LAT, 0)
    tables = (cycle_offsets, lon_shifts, basis_ids)
    distant = lax.ppermute(own, LAT, off_chip)
    beside = lax.ppermute(own, LAT, on_chip)
    summed, coefs = own_terms(tables, entry_values, own, wide)
    activated, grad_pre, partial_w = mix(
        tables, coefs, distant, beside, summed, flat_weights, cotangent[0, 0]
    )

    pieces = lax.all_to_all(
        partial_w.reshape(lax.axis_size(NEAR), -1, channels), NEAR, 0, 0
    )
    to_distant, middle, to_beside = backward(tables, coefs, grad_pre, flat_weights)
    from_distant = lax.ppermute(to_distant, LAT, off_chip)
    from_beside = lax.ppermute(to_beside, LAT, on_chip)
    chunk = pieces.astype(F32).sum(0).astype(BF16)
    chunk, _ = lax.optimization_barrier((chunk, to_beside))
    pieces = to_all(chunk, FAR)
    field_gradient = (middle + from_distant.astype(F32) + from_beside.astype(F32)).astype(BF16)
    cell_count = lax.axis_size(LAT) * lax.axis_size(ENS) * lon_count
    chunk = (pieces.astype(F32).sum(0) * (1.0 / math.sqrt(cell_count))).astype(BF16)
    chunk, field_gradient = lax.optimization_barrier((chunk, field_gradient))
    pieces = to_all(chunk, NEAR)
    grad_weights = pieces.reshape(weights.shape).astype(F32)
    return (activated[None, None], field_gradient[None, None], grad_weights)


def solution(mesh):
    lat_count, ens_count = mesh.devices.shape
    grid = Mesh(
        np.asarray(mesh.devices).reshape(lat_count // 4, 2, 2, 4, ens_count // 4),
        LAT + ENS,
    )
    placed = (
        P(ENS, LAT, None, None),
        P(ENS, LAT, None, None),
        P(),
        P(LAT, None),
        P(LAT, None),
        P(LAT, None),
        P(LAT, None),
    )
    return jax.shard_map(
        on_device,
        mesh=grid,
        in_specs=placed,
        out_specs=(P(ENS, LAT, None, None), P(ENS, LAT, None, None), P()),
        check_vma=False,
    )
```

time: 86.8 us -> 84.4 us (0.972)
  starting transfers between devices: 34 us -> 37.1 us
  waiting for transfers between devices: 17.2 us -> 14.5 us
  Pallas kernels: 11.5 us -> 10.1 us
  local copies, waits for them, and re-layouts: 2.32 us -> 1.32 us
    ppermute x1, starting transfers between devices: 8.92 us -> 4.54 us  [on_device(): beside = lax.ppermute(own, LAT, on_chip)]
    all_to_all x2, starting transfers between devices: 18.3 us -> 22.1 us  [the longest x1 14.3 us: to_all(): lax.all_to_all(jnp.broadcast_to(block[None], (count,) + block.shape), axe...]
    ppermute x1, starting transfers between devices: 1.92 us -> 4.94 us  [on_device(): distant = lax.ppermute(own, LAT, off_chip)]
    unnamed x16 -> x2, local copies, waits for them, and re-layouts: 2.32 us -> 0.65 us
    ppermute x1, waiting for transfers between devices: 1.58 us -> 0.01 us  [on_device(): distant = lax.ppermute(own, LAT, off_chip)]
    all_to_all x2, waiting for transfers between devices: 15.6 us -> 14.5 us  [the longest x1 12 us: to_all(): lax.all_to_all(jnp.broadcast_to(block[None], (count,) + block.shape), axe...]
    pallas_call x3 -> x1, Pallas kernels: 2.65 us -> 1.54 us  [own_terms(): pl.pallas_call(own_kernel, out_shape=(shape((wide // LANES, lon_count, LA...]
  transfers between devices with their start and end apart: 6 -> 6, of which waited for: 3 -> 2; matrix products, arithmetic and copies ran while one was open for 2% -> 2% of each run, Pallas kernels for 7% -> 6%
where the time goes in v3:
time: 84.4 us; the launch traced here: 84 us
  starting transfers between devices  37.1 us (44%)
  blocking collectives  18.2 us (22%)
  waiting for transfers between devices  14.5 us (17%)
  Pallas kernels  10.1 us (12%)
  other arithmetic  2.05 us (2%)
  local copies, waits for them, and re-layouts  1.32 us (2%)
    all_to_all x1, blocking collectives, to_all(): lax.all_to_all(jnp.broadcast_to(block[None], (count,) + block.shape), axe...  18.2 us
    all_to_all x1, starting transfers between devices, to_all(): lax.all_to_all(jnp.broadcast_to(block[None], (count,) + block.shape), axe...  14.3 us
    all_to_all x1, waiting for transfers between devices, to_all(): lax.all_to_all(jnp.broadcast_to(block[None], (count,) + block.shape), axe...  12 us
    all_to_all x1, starting transfers between devices, on_device(): lax.all_to_all(partial_w.reshape(lax.axis_size(NEAR), -1, channels), NEAR...  7.71 us
    pallas_call x1, Pallas kernels, mix(): pl.pallas_call(mix_kernel, out_shape=(shape((lon_count, channels), BF16),...  4.98 us
    ppermute x1, starting transfers between devices, on_device(): distant = lax.ppermute(own, LAT, off_chip)  4.94 us
    ppermute x1, starting transfers between devices, on_device(): beside = lax.ppermute(own, LAT, on_chip)  4.54 us
    ppermute x1, starting transfers between devices, on_device(): from_distant = lax.ppermute(to_distant, LAT, off_chip)  3.65 us
  transfers between devices with their start and end apart: 6, of which 2 were waited for; matrix products, arithmetic and copies ran while one was open for 2% of the time, Pallas kernels for 6%

profile of v3, /device:TPU:1, one launch (start us, length us, event | category | flops | bytes accessed | tf_op | source)
XLA Modules:
  0.0 84.0 jit_solution(12436156932622142465)
XLA Ops:
  0.6 4.9 %collective-permute-start.1 = (bf16[720,256]{1,0:T(8,128)(2,1)}, bf16[720,256]{1,0:T(8,128)(2,1)S(1)}, u32[]{:S(2)}, u32[]{:S(2)}) collective-permute-start(bf16[720,256]{1,0:T(8,128)(2,1)} %bitcast.14), channel_id=1, source_target_pairs={{16,32},{48,64},{80,96},{112,128},{144,160},{176,192},{208,224},{2... | collective-permute-start | bytes 1105928 | tf_op jit(solution)/shard_map/ppermute | solution.py:318
  5.6 4.5 %collective-permute-start = (bf16[720,256]{1,0:T(8,128)(2,1)}, bf16[720,256]{1,0:T(8,128)(2,1)S(1)}, u32[]{:S(2)}, u32[]{:S(2)}) collective-permute-start(bf16[720,256]{1,0:T(8,128)(2,1)} %bitcast.15), channel_id=1, source_target_pairs={{0,16},{32,48},{64,80},{96,112},{128,144},{160,176},{192,208},{224... | collective-permute-start | bytes 1105928 | tf_op jit(solution)/shard_map/ppermute | solution.py:319
  10.1 0.0 copy-start
  10.1 0.6 copy-done
  10.8 1.5 %own_terms.1 = (f32[8,720,128]{2,1,0:T(8,128)S(1)}, f32[16,128]{1,0:T(8,128)S(1)}) custom-call(s32[1,16]{1,0:T(1,128)} %offsets_hbm.5, s32[1,16]{1,0:T(1,128)} %shifts_hbm.5, s32[1,16]{1,0:T(1,128)} %basis_ids_hbm.5, bf16[1,16]{1,0:T(2,128)(2,1)S(1)} %copy-done, bf16[720,256]{1,0:T(8,128)(2,1)} %bitcast.16), custom_call_target="tpu_custom_call" | custom-call | bytes 4194304 | tf_op jit(solution)/shard_map/own_terms/pallas_call | solution.py:226
  12.3 0.0 collective-permute-done.1.distant
  12.3 0.0 collective-permute-done.beside
  12.3 5.0 %mix.1 = (bf16[720,256]{1,0:T(8,128)(2,1)}, bf16[720,256]{1,0:T(8,128)(2,1)S(1)}, bf16[1024,256]{1,0:T(8,128)(2,1)}, f32[8,720,128]{2,1,0:T(8,128)S(1)}) custom-call(s32[1,16]{1,0:T(1,128)} %offsets_hbm.5, s32[1,16]{1,0:T(1,128)} %shifts_hbm.5, s32[1,16]{1,0:T(1,128)} %basis_ids_hbm.5, ...), custom_call_target="tpu_custom_call", output_to_operand_aliasing={{3}: (6, {})} | custom-call | flops 754974720 | bytes 8388608 | tf_op jit(solution)/shard_map/mix/pallas_call | solution.py:251
  17.3 7.7 %all-to-all-start = ((bf16[64,16,256]{2,1,0:T(8,128)(2,1)}), bf16[64,16,256]{2,1,0:T(8,128)(2,1)S(1)}, u32[]{:S(2)}, u32[]{:S(2)}) async-start(bf16[64,16,256]{2,1,0:T(8,128)(2,1)} %bitcast.4), calls=%async_computation | async-start | bytes 1048576 | tf_op jit(solution)/shard_map/all_to_all | solution.py:325
  25.1 3.6 %backward.1 = (bf16[720,256]{1,0:T(8,128)(2,1)S(1)}, f32[720,256]{1,0:T(8,128)S(1)}, bf16[720,256]{1,0:T(8,128)(2,1)S(1)}) custom-call(s32[1,16]{1,0:T(1,128)} %offsets_hbm.5, s32[1,16]{1,0:T(1,128)} %shifts_hbm.5, s32[1,16]{1,0:T(1,128)} %basis_ids_hbm.5, f32[16,128]{1,0:T(8,128)S(1)} %get-tuple-element.14.coefs, ...), custom_call_target="tpu_custom_call" | custom-call | flops 377487360 | bytes 8388608 | tf_op jit(solution)/shard_map/backward/pallas_call | solution.py:283
  28.6 3.6 %collective-permute-start.2 = (bf16[720,256]{1,0:T(8,128)(2,1)S(1)}, bf16[720,256]{1,0:T(8,128)(2,1)S(1)}, u32[]{:S(2)}, u32[]{:S(2)}) collective-permute-start(bf16[720,256]{1,0:T(8,128)(2,1)S(1)} %get-tuple-element.22), channel_id=1, source_target_pairs={{16,32},{48,64},{80,96},{112,128},{144,160},{176,192},{208,224},{2... | collective-permute-start | bytes 1105928 | tf_op jit(solution)/shard_map/ppermute | solution.py:329
  32.3 1.9 %collective-permute-start.3 = (bf16[720,256]{1,0:T(8,128)(2,1)S(1)}, bf16[720,256]{1,0:T(8,128)(2,1)S(1)}, u32[]{:S(2)}, u32[]{:S(2)}) collective-permute-start(bf16[720,256]{1,0:T(8,128)(2,1)S(1)} %get-tuple-element.19), channel_id=1, source_target_pairs={{0,16},{32,48},{64,80},{96,112},{128,144},{160,176},{192,208},{224... | collective-permute-start | bytes 1105928 | tf_op jit(solution)/shard_map/ppermute | solution.py:330
  34.2 2.4 %all-to-all-done = bf16[64,16,256]{2,1,0:T(8,128)(2,1)S(1)} async-done(((bf16[64,16,256]{2,1,0:T(8,128)(2,1)}), bf16[64,16,256]{2,1,0:T(8,128)(2,1)S(1)}, u32[]{:S(2)}, u32[]{:S(2)}) %all-to-all-start) | async-done | bytes 524320 | tf_op jit(solution)/shard_map/all_to_all | solution.py:325
  36.6 0.1 reduce_sum.21
  36.7 0.6 broadcast_in_dim.9
  37.4 14.3 %all-to-all-start.1 = ((bf16[8,16,256]{2,1,0:T(8,128)(2,1)}), bf16[8,16,256]{2,1,0:T(8,128)(2,1)S(1)}, u32[]{:S(2)}, u32[]{:S(2)}) async-start(bf16[8,16,256]{2,1,0:T(8,128)(2,1)} %broadcast_in_dim.9), calls=%async_computation.1 | async-start | bytes 131072 | tf_op jit(solution)/shard_map/all_to_all | solution.py:307
  51.7 0.0 collective-permute-done.2
  51.7 0.0 collective-permute-done.3
  51.7 0.9 %add_convert_fusion = bf16[720,256]{1,0:T(8,128)(2,1)} fusion(bf16[720,256]{1,0:T(8,128)(2,1)S(1)} %collective-permute-done.3, f32[720,256]{1,0:T(8,128)S(1)} %get-tuple-element.21, bf16[720,256]{1,0:T(8,128)(2,1)S(1)} %collective-permute-done.2), kind=kLoop, calls=%fused_computation | loop fusion | flops 921600 | bytes 1843200 | tf_op jit(solution)/shard_map/convert_element_type | solution.py:334
  52.6 12.0 %all-to-all-done.1 = bf16[8,16,256]{2,1,0:T(8,128)(2,1)S(1)} async-done(((bf16[8,16,256]{2,1,0:T(8,128)(2,1)}), bf16[8,16,256]{2,1,0:T(8,128)(2,1)S(1)}, u32[]{:S(2)}, u32[]{:S(2)}) %all-to-all-start.1) | async-done | bytes 65568 | tf_op jit(solution)/shard_map/all_to_all | solution.py:307
  64.7 18.2 %all_to_all.15 = bf16[64,16,256]{2,1,0:T(8,128)(2,1)S(1)} all-to-all(bf16[64,16,256]{2,1,0:T(8,128)(2,1)S(1)} %broadcast_in_dim.21), channel_id=1, replica_groups=mesh['za'=8,'zp'=2,'core'=2,'x'=4,'y'=4] {'zp','core','x','y'}, dimensions={0} | all-to-all | bytes 1048576 | tf_op jit(solution)/shard_map/all_to_all | solution.py:307
  82.9 1.1 %bitcast_convert_fusion = f32[4,256,256]{2,1,0:T(8,128)} fusion(bf16[4,256,256]{2,1,0:T(8,128)(2,1)S(1)} %bitcast.10), kind=kLoop, calls=%fused_computation.1 | loop fusion | flops 262144 | bytes 1572864 | tf_op jit(solution)/shard_map/convert_element_type | solution.py:339
  (3 shorter events, 0.1 us)
Async XLA Ops:
  0.6 11.7 %collective-permute-start.1 = (bf16[720,256]{1,0:T(8,128)(2,1)}, bf16[720,256]{1,0:T(8,128)(2,1)S(1)}, u32[]{:S(2)}, u32[]{:S(2)}) collective-permute-start(bf16[720,256]{1,0:T(8,128)(2,1)} %bitcast.14), channel_id=1, source_target_pairs={{16,32},{48,64},{80,96},{112,128},{144,160},{176,192},{208,224},{2... | collective-permute-start | bytes 1105928 | tf_op jit(solution)/shard_map/ppermute | solution.py:318
  5.6 6.8 %collective-permute-start = (bf16[720,256]{1,0:T(8,128)(2,1)}, bf16[720,256]{1,0:T(8,128)(2,1)S(1)}, u32[]{:S(2)}, u32[]{:S(2)}) collective-permute-start(bf16[720,256]{1,0:T(8,128)(2,1)} %bitcast.15), channel_id=1, source_target_pairs={{0,16},{32,48},{64,80},{96,112},{128,144},{160,176},{192,208},{224... | collective-permute-start | bytes 1105928 | tf_op jit(solution)/shard_map/ppermute | solution.py:319
  10.1 0.7 copy-start
  17.3 19.3 %all-to-all-start = ((bf16[64,16,256]{2,1,0:T(8,128)(2,1)}), bf16[64,16,256]{2,1,0:T(8,128)(2,1)S(1)}, u32[]{:S(2)}, u32[]{:S(2)}) async-start(bf16[64,16,256]{2,1,0:T(8,128)(2,1)} %bitcast.4), calls=%async_computation | async-start | bytes 1048576 | tf_op jit(solution)/shard_map/all_to_all | solution.py:325
  28.6 23.1 %collective-permute-start.2 = (bf16[720,256]{1,0:T(8,128)(2,1)S(1)}, bf16[720,256]{1,0:T(8,128)(2,1)S(1)}, u32[]{:S(2)}, u32[]{:S(2)}) collective-permute-start(bf16[720,256]{1,0:T(8,128)(2,1)S(1)} %get-tuple-element.22), channel_id=1, source_target_pairs={{16,32},{48,64},{80,96},{112,128},{144,160},{176,192},{208,224},{2... | collective-permute-start | bytes 1105928 | tf_op jit(solution)/shard_map/ppermute | solution.py:329
  32.3 19.4 %collective-permute-start.3 = (bf16[720,256]{1,0:T(8,128)(2,1)S(1)}, bf16[720,256]{1,0:T(8,128)(2,1)S(1)}, u32[]{:S(2)}, u32[]{:S(2)}) collective-permute-start(bf16[720,256]{1,0:T(8,128)(2,1)S(1)} %get-tuple-element.19), channel_id=1, source_target_pairs={{0,16},{32,48},{64,80},{96,112},{128,144},{160,176},{192,208},{224... | collective-permute-start | bytes 1105928 | tf_op jit(solution)/shard_map/ppermute | solution.py:330
  37.4 27.3 %all-to-all-start.1 = ((bf16[8,16,256]{2,1,0:T(8,128)(2,1)}), bf16[8,16,256]{2,1,0:T(8,128)(2,1)S(1)}, u32[]{:S(2)}, u32[]{:S(2)}) async-start(bf16[8,16,256]{2,1,0:T(8,128)(2,1)} %broadcast_in_dim.9), calls=%async_computation.1 | async-start | bytes 131072 | tf_op jit(solution)/shard_map/all_to_all | solution.py:307

commit v4 on v3

--- a/solution.py
+++ b/solution.py
@@ -13,7 +13,11 @@
 F32 = jnp.float32
 LANES = 128
 SLAB = 48
-PARTS = 3
+PARTS = 5
+TOGETHER = 4
+ENTRY_UNIT = 1 << 16
+SLOT_UNIT = 1 << 12
+PLAN = 128
 VMEM_BYTES = 48 * 1024 * 1024
 LAT = ("za", "zp", "core")
 ENS = ("x", "y")
@@ -48,7 +52,64 @@
     row = lax.broadcasted_iota(jnp.int32, (count, count), 0)
     column = lax.broadcasted_iota(jnp.int32, (count, count), 1)
     picked = jnp.sum(jnp.where(row == column, wide, 0.0), axis=1, keepdims=True)
-    rows[...] = jnp.broadcast_to(picked, rows.shape)
+    rows[...] = jnp.zeros_like(rows)
+    rows[0:count, :] = jnp.broadcast_to(picked, (count, rows.shape[1]))
+
+
+def list_room(entry_count):
+    return -(-entry_count // TOGETHER) * TOGETHER
+
+
+def plan_entries(plan, offsets, shifts, basis_ids, lon_count, basis_count):
+    entry_count = offsets.shape[1]
+    room = list_room(entry_count)
+    groups = basis_count + 3
+    counts = groups * room
+
+    def clear(i, carry):
+        plan[0, i] = jnp.where(i < counts, entry_count * ENTRY_UNIT, 0)
+        return carry
+
+    lax.fori_loop(0, counts + groups, clear, 0)
+    turn = 1 - 2 * lax.axis_index("core")
+
+    def note(group, code):
+        place = plan[0, counts + group]
+        plan[0, group * room + place] = code
+        plan[0, counts + group] = place + 1
+
+    def add_entry(entry, carry):
+        side = offsets[0, entry] * turn
+        basis = basis_ids[0, entry]
+        shift = shifts[0, entry]
+
+        @pl.when(side != 0)
+        def _():
+            slot = jnp.where(side > 0, SLOT_UNIT, 0)
+            note(basis, entry * ENTRY_UNIT + slot + shift)
+
+        note(basis_count + 1 + side, entry * ENTRY_UNIT + basis * SLOT_UNIT + lon_count - shift)
+        return carry
+
+    lax.fori_loop(0, entry_count, add_entry, 0)
+
+
+def passes_of(plan, group, groups, room):
+    return (plan[0, groups * room + group] + (TOGETHER - 1)) // TOGETHER
+
+
+def few_terms(plan, first, coefs, slabs, lon_count, halves):
+    terms = [None] * halves
+    for i in range(TOGETHER):
+        code = plan[0, first + i]
+        entry = lax.shift_right_logical(code, 16)
+        slot = (lax.shift_right_logical(code, 12) & 15) * halves
+        start = code & (SLOT_UNIT - 1)
+        value = coefs[pl.ds(entry, 1), :]
+        for half in range(halves):
+            term = value * slabs[slot + half, pl.ds(start, lon_count), :]
+            terms[half] = term if i == 0 else terms[half] + term
+    return terms
 
 
 def add_rows(total, source, value, halves, target, slot, start):
@@ -58,17 +119,25 @@
 
 
 def own_kernel(
-    offsets_hbm, shifts_hbm, basis_ids_hbm, values, own_hbm, summed, coefs,
-    offsets, shifts, basis_ids, own, slabs, arrived,
+    offsets_hbm, shifts_hbm, basis_ids_hbm, values, own_hbm, weights_hbm, cotangent_hbm,
+    summed, coefs, plan_out, weights, cotangent,
+    offsets, shifts, basis_ids, plan, own, slabs, arrived, left,
 ):
     halves = own.shape[1] // LANES
     copies = fetched(
-        (offsets_hbm, shifts_hbm, basis_ids_hbm, own_hbm), (offsets, shifts, basis_ids, own), arrived
+        (offsets_hbm, shifts_hbm, basis_ids_hbm, own_hbm, weights_hbm, cotangent_hbm),
+        (offsets, shifts, basis_ids, own, weights, cotangent),
+        arrived,
     )
     spread(values, coefs)
     summed[...] = jnp.zeros_like(summed)
-    for copy in copies:
+    for copy in copies[:4]:
         copy.wait()
+    plan_entries(
+        plan, offsets, shifts, basis_ids, own.shape[0], summed.shape[0] // halves
+    )
+    put_plan = pltpu.make_async_copy(plan, plan_out, left)
+    put_plan.start()
     fill_twice(slabs, 0, own[...].astype(F32))
 
     def add_entry(entry, carry):
@@ -82,50 +151,45 @@
         return carry
 
     lax.fori_loop(0, offsets.shape[1], add_entry, 0)
+    put_plan.wait()
+    for copy in copies[4:]:
+        copy.wait()
 
 
 def mix_kernel(
-    offsets_hbm, shifts_hbm, basis_ids_hbm, coefs, beside, distant, summed_in, weights_hbm, cotangent_hbm,
+    plan_in, coefs, beside, distant, summed_in, weights, cotangent,
     activated_hbm, grad_pre, partial_w_hbm, summed,
-    offsets, shifts, basis_ids, slabs, basis, weights, cotangent, activated, partial_w,
-    arrived, left,
+    plan, slabs, basis, activated, partial_w, arrived, left,
 ):
     del summed_in
     lon_count, channels = distant.shape
     halves = channels // LANES
     basis_count = weights.shape[0] // channels
-    copies = fetched(
-        (offsets_hbm, shifts_hbm, basis_ids_hbm, weights_hbm, cotangent_hbm),
-        (offsets, shifts, basis_ids, weights, cotangent),
-        arrived,
-    )
-    for copy in copies[:3]:
-        copy.wait()
+    get_plan = pltpu.make_async_copy(plan_in, plan, arrived)
+    get_plan.start()
     fill_twice(slabs, 0, distant[...].astype(F32))
     fill_twice(slabs, halves, beside[...].astype(F32))
-    turn = 1 - 2 * lax.axis_index("core")
-
-    def add_entry(entry, carry):
-        side = offsets[0, entry] * turn
-
-        @pl.when(side != 0)
-        def _():
-            add_rows(
-                summed, slabs, coefs[pl.ds(entry, 1), :], halves,
-                basis_ids[0, entry] * halves, (side + 1) // 2 * halves, shifts[0, entry],
-            )
-
-        return carry
-
-    lax.fori_loop(0, offsets.shape[1], add_entry, 0)
-    copies[3].wait()
-    copies[4].wait()
+    get_plan.wait()
+    groups, room = basis_count + 3, list_room(coefs.shape[0] - 8)
+    for k in range(basis_count):
+        passes = passes_of(plan, k, groups, room)
+
+        def add_pass(i, carry):
+            terms = few_terms(plan, k * room + i * TOGETHER, coefs, slabs, lon_count, halves)
+            for half in range(halves):
+                summed[k * halves + half] += terms[half]
+            return carry
+
+        last = jnp.maximum(passes - 1, 0)
+        lax.fori_loop(0, last, add_pass, 0)
+        terms = few_terms(plan, k * room + last * TOGETHER, coefs, slabs, lon_count, halves)
+        for half in range(halves):
+            column = k * halves + half
+            basis[:, column * LANES : (column + 1) * LANES] = (summed[column] + terms[half]).astype(BF16)
     root = math.sqrt(2.0 / math.pi)
     part = lon_count // PARTS
     for first in range(0, lon_count, part):
         rows = slice(first, first + part)
-        for column in range(basis_count * halves):
-            basis[rows, column * LANES : (column + 1) * LANES] = summed[column, rows, :].astype(BF16)
         preact = jnp.dot(basis[rows, :], weights[...], preferred_element_type=F32)
         for slab in range(0, part, SLAB):
             v = preact[slab : slab + SLAB]
@@ -154,20 +218,14 @@
 
 
 def backward_kernel(
-    offsets_hbm, shifts_hbm, basis_ids_hbm, coefs, grad_pre, weights_hbm, distant, own, beside,
-    offsets, shifts, basis_ids, weights, slabs, summed, arrived,
+    plan_in, coefs, grad_pre, weights, distant, own, beside,
+    plan, slabs, summed, arrived,
 ):
     lon_count, channels = grad_pre.shape
     halves = channels // LANES
     basis_count = weights.shape[0] // channels
-    copies = fetched(
-        (offsets_hbm, shifts_hbm, basis_ids_hbm, weights_hbm),
-        (offsets, shifts, basis_ids, weights),
-        arrived,
-    )
-    summed[...] = jnp.zeros_like(summed)
-    for copy in copies:
-        copy.wait()
+    get_plan = pltpu.make_async_copy(plan_in, plan, arrived)
+    get_plan.start()
     for k in range(basis_count):
         product = lax.dot_general(
             grad_pre[...],
@@ -176,20 +234,35 @@
             preferred_element_type=F32,
         )
         fill_twice(slabs, k * halves, product.astype(BF16).astype(F32))
-    turn = 1 - 2 * lax.axis_index("core")
-
-    def add_entry(entry, carry):
-        add_rows(
-            summed, slabs, coefs[pl.ds(entry, 1), :], halves,
-            (offsets[0, entry] * turn + 1) * halves, basis_ids[0, entry] * halves,
-            lon_count - shifts[0, entry],
-        )
-        return carry
-
-    lax.fori_loop(0, offsets.shape[1], add_entry, 0)
-    for slot, out in enumerate((distant, own, beside)):
-        for half in range(halves):
-            out[:, half * LANES : (half + 1) * LANES] = summed[slot * halves + half].astype(out.dtype)
+    get_plan.wait()
+    groups, room = basis_count + 3, list_room(coefs.shape[0] - 8)
+    for side, out in enumerate((distant, own, beside)):
+        group = basis_count + side
+        passes = passes_of(plan, group, groups, room)
+
+        def terms_of(i):
+            return few_terms(plan, group * room + i * TOGETHER, coefs, slabs, lon_count, halves)
+
+        def put(terms):
+            for half in range(halves):
+                out[:, half * LANES : (half + 1) * LANES] = terms[half].astype(out.dtype)
+
+        @pl.when(passes <= 1)
+        def _():
+            put(terms_of(0))
+
+        @pl.when(passes > 1)
+        def _():
+            for half, term in enumerate(terms_of(0)):
+                summed[half] = term
+
+            def add_pass(i, carry):
+                for half, term in enumerate(terms_of(i)):
+                    summed[half] += term
+                return carry
+
+            lax.fori_loop(1, passes - 1, add_pass, 0)
+            put([summed[half] + term for half, term in enumerate(terms_of(passes - 1))])
 
 
 def vmem():
@@ -204,6 +277,10 @@
     return [pltpu.with_memory_space_constraint(array, pltpu.HBM) for array in arrays]
 
 
+def either():
+    return pl.BlockSpec(memory_space=pl.ANY)
+
+
 def params():
     return pltpu.CompilerParams(vmem_limit_bytes=VMEM_BYTES)
 
@@ -220,30 +297,36 @@
     return [pltpu.SMEM((1, entry_count), jnp.int32)] * 3
 
 
-def own_terms(tables, values, own, wide):
+def own_terms(tables, values, own, weights, cotangent):
     lon_count, channels = own.shape
+    wide = weights.shape[0]
     entry_count = values.shape[1]
     return pl.pallas_call(
         own_kernel,
         out_shape=(
             shape((wide // LANES, lon_count, LANES), F32),
-            shape((entry_count, LANES), F32),
+            shape((entry_count + 8, LANES), F32),
+            shape((1, PLAN), jnp.int32),
+            shape(weights.shape, BF16),
+            shape(cotangent.shape, BF16),
         ),
-        in_specs=[hbm()] * 3 + [vmem(), hbm()],
-        out_specs=(vmem(), vmem()),
-        scratch_shapes=table_scratch(entry_count)
+        in_specs=[hbm()] * 3 + [vmem()] + [hbm()] * 3,
+        out_specs=(vmem(), vmem(), either(), vmem(), vmem()),
+        scratch_shapes=[pltpu.SMEM((1, entry_count), jnp.int32)] * 3
         + [
+            pltpu.SMEM((1, PLAN), jnp.int32),
             pltpu.VMEM((lon_count, channels), BF16),
             pltpu.VMEM((channels // LANES, 2 * lon_count, LANES), F32),
-            pltpu.SemaphoreType.DMA((4,)),
+            pltpu.SemaphoreType.DMA((6,)),
+            pltpu.SemaphoreType.DMA,
         ],
         compiler_params=params(),
         cost_estimate=cost(0, 4),
         name="own_terms",
-    )(*kept_out(tables), values, *kept_out([own]))
-
-
-def mix(tables, coefs, distant, beside, summed, weights, cotangent):
+    )(*kept_out(tables), values, *kept_out([own, weights, cotangent]))
+
+
+def mix(plan, coefs, distant, beside, summed, weights, cotangent):
     lon_count, channels = distant.shape
     wide = weights.shape[0]
     field = pltpu.VMEM((lon_count, channels), BF16)
@@ -256,29 +339,26 @@
             shape((wide, channels), BF16),
             shape(summed.shape, F32),
         ),
-        in_specs=[hbm()] * 3 + [vmem()] * 4 + [hbm()] * 2,
+        in_specs=[either()] + [vmem()] * 6,
         out_specs=(hbm(), vmem(), hbm(), vmem()),
-        input_output_aliases={6: 3},
-        scratch_shapes=table_scratch(coefs.shape[0])
-        + [
+        input_output_aliases={4: 3},
+        scratch_shapes=[
+            pltpu.SMEM((1, PLAN), jnp.int32),
             pltpu.VMEM((2 * channels // LANES, 2 * lon_count, LANES), F32),
             pltpu.VMEM((lon_count, wide), BF16),
-            square,
-            field,
             field,
             square,
-            pltpu.SemaphoreType.DMA((5,)),
+            pltpu.SemaphoreType.DMA,
             pltpu.SemaphoreType.DMA((wide // channels + 1,)),
         ],
         compiler_params=params(),
         cost_estimate=cost(4 * lon_count * wide * channels, 8),
         name="mix",
-    )(*kept_out(tables), coefs, beside, distant, summed, *kept_out([weights, cotangent]))[:3]
-
-
-def backward(tables, coefs, grad_pre, weights):
+    )(plan, coefs, beside, distant, summed, weights, cotangent)[:3]
+
+
+def backward(plan, coefs, grad_pre, weights):
     lon_count, channels = grad_pre.shape
-    halves = channels // LANES
     wide = weights.shape[0]
     return pl.pallas_call(
         backward_kernel,
@@ -287,19 +367,18 @@
             shape((lon_count, channels), F32),
             shape((lon_count, channels), BF16),
         ),
-        in_specs=[hbm()] * 3 + [vmem()] * 2 + [hbm()],
+        in_specs=[either()] + [vmem()] * 3,
         out_specs=(vmem(), vmem(), vmem()),
-        scratch_shapes=table_scratch(coefs.shape[0])
-        + [
-            pltpu.VMEM((wide, channels), BF16),
+        scratch_shapes=[
+            pltpu.SMEM((1, PLAN), jnp.int32),
             pltpu.VMEM((wide // LANES, 2 * lon_count, LANES), F32),
-            pltpu.VMEM((3 * halves, lon_count, LANES), F32),
-            pltpu.SemaphoreType.DMA((4,)),
+            pltpu.VMEM((channels // LANES, lon_count, LANES), F32),
+            pltpu.SemaphoreType.DMA,
         ],
         compiler_params=params(),
         cost_estimate=cost(2 * lon_count * wide * channels, 8),
         name="backward",
-    )(*kept_out(tables), coefs, grad_pre, *kept_out([weights]))
+    )(plan, coefs, grad_pre, weights)
 
 
 def to_all(block, axes):
@@ -312,20 +391,21 @@
     lon_count, channels = own.shape
     basis_count = weights.shape[0]
     wide = basis_count * channels
-    flat_weights = weights.reshape(wide, channels)
     off_chip, on_chip = pair_swap(LAT, 1), pair_swap(LAT, 0)
     tables = (cycle_offsets, lon_shifts, basis_ids)
     distant = lax.ppermute(own, LAT, off_chip)
     beside = lax.ppermute(own, LAT, on_chip)
-    summed, coefs = own_terms(tables, entry_values, own, wide)
+    summed, coefs, plan, flat_weights, cotangent = own_terms(
+        tables, entry_values, own, weights.reshape(wide, channels), cotangent[0, 0]
+    )
     activated, grad_pre, partial_w = mix(
-        tables, coefs, distant, beside, summed, flat_weights, cotangent[0, 0]
+        plan, coefs, distant, beside, summed, flat_weights, cotangent
     )
 
     pieces = lax.all_to_all(
         partial_w.reshape(lax.axis_size(NEAR), -1, channels), NEAR, 0, 0
     )
-    to_distant, middle, to_beside = backward(tables, coefs, grad_pre, flat_weights)
+    to_distant, middle, to_beside = backward(plan, coefs, grad_pre, flat_weights)
     from_distant = lax.ppermute(to_distant, LAT, off_chip)
     from_beside = lax.ppermute(to_beside, LAT, on_chip)
     chunk = pieces.astype(F32).sum(0).astype(BF16)

time: 84.4 us -> 83.3 us (0.987)
  waiting for transfers between devices: 14.5 us -> 16 us
  Pallas kernels: 10.1 us -> 8.91 us
  starting transfers between devices: 37.1 us -> 36.1 us
    all_to_all x1, waiting for transfers between devices: 2.41 us -> 3.93 us  [on_device(): lax.all_to_all(partial_w.reshape(lax.axis_size(NEAR), -1, channels), NEAR...]
    pallas_call x1, Pallas kernels: 3.58 us -> 2.11 us  [backward(): pl.pallas_call(backward_kernel, out_shape=(shape((lon_count, channels), B...]
    pallas_call x1, Pallas kernels: 1.54 us -> 2.94 us  [own_terms(): pl.pallas_call(own_kernel, out_shape=(shape((wide // LANES, lon_count, LA...]
    pallas_call x1, Pallas kernels: 4.98 us -> 3.86 us  [mix(): pl.pallas_call(mix_kernel, out_shape=(shape((lon_count, channels), BF16),...]
    all_to_all x1, starting transfers between devices: 7.71 us -> 6.81 us  [on_device(): lax.all_to_all(partial_w.reshape(lax.axis_size(NEAR), -1, channels), NEAR...]
where the time goes in v4:
time: 83.3 us; the launch traced here: 82.8 us
  starting transfers between devices  36.1 us (43%)
  blocking collectives  17.7 us (21%)
  waiting for transfers between devices  16 us (19%)
  Pallas kernels  8.91 us (11%)
  other arithmetic  2.03 us (2%)
  local copies, waits for them, and re-layouts  1.32 us (2%)
    all_to_all x1, blocking collectives, to_all(): lax.all_to_all(jnp.broadcast_to(block[None], (count,) + block.shape), axe...  17.7 us
    all_to_all x1, starting transfers between devices, to_all(): lax.all_to_all(jnp.broadcast_to(block[None], (count,) + block.shape), axe...  14.3 us
    all_to_all x1, waiting for transfers between devices, to_all(): lax.all_to_all(jnp.broadcast_to(block[None], (count,) + block.shape), axe...  12.1 us
    all_to_all x1, starting transfers between devices, on_device(): lax.all_to_all(partial_w.reshape(lax.axis_size(NEAR), -1, channels), NEAR...  6.81 us
    ppermute x1, starting transfers between devices, on_device(): distant = lax.ppermute(own, LAT, off_chip)  4.94 us
    ppermute x1, starting transfers between devices, on_device(): beside = lax.ppermute(own, LAT, on_chip)  4.54 us
    all_to_all x1, waiting for transfers between devices, on_device(): lax.all_to_all(partial_w.reshape(lax.axis_size(NEAR), -1, channels), NEAR...  3.93 us
    pallas_call x1, Pallas kernels, mix(): pl.pallas_call(mix_kernel, out_shape=(shape((lon_count, channels), BF16),...  3.86 us
  transfers between devices with their start and end apart: 6, of which 2 were waited for; matrix products, arithmetic and copies ran while one was open for 2% of the time, Pallas kernels for 6%

profile of v4, /device:TPU:1, one launch (start us, length us, event | category | flops | bytes accessed | tf_op | source)
XLA Modules:
  0.0 82.8 jit_solution(8471547627691753367)
XLA Ops:
  0.6 4.9 %collective-permute-start.1 = (bf16[720,256]{1,0:T(8,128)(2,1)}, bf16[720,256]{1,0:T(8,128)(2,1)S(1)}, u32[]{:S(2)}, u32[]{:S(2)}) collective-permute-start(bf16[720,256]{1,0:T(8,128)(2,1)} %bitcast.14), channel_id=1, source_target_pairs={{16,32},{48,64},{80,96},{112,128},{144,160},{176,192},{208,224},{2... | collective-permute-start | bytes 1105928 | tf_op jit(solution)/shard_map/ppermute | solution.py:396
  5.6 4.5 %collective-permute-start = (bf16[720,256]{1,0:T(8,128)(2,1)}, bf16[720,256]{1,0:T(8,128)(2,1)S(1)}, u32[]{:S(2)}, u32[]{:S(2)}) collective-permute-start(bf16[720,256]{1,0:T(8,128)(2,1)} %bitcast.15), channel_id=1, source_target_pairs={{0,16},{32,48},{64,80},{96,112},{128,144},{160,176},{192,208},{224... | collective-permute-start | bytes 1105928 | tf_op jit(solution)/shard_map/ppermute | solution.py:397
  10.1 0.0 copy-start
  10.1 0.6 copy-done
  10.8 2.9 %own_terms.1 = (f32[8,720,128]{2,1,0:T(8,128)S(1)}, f32[24,128]{1,0:T(8,128)S(1)}, s32[1,128]{1,0:T(1,128)S(1)}, bf16[1024,256]{1,0:T(8,128)(2,1)S(1)}, bf16[720,256]{1,0:T(8,128)(2,1)S(1)}) custom-call(s32[1,16]{1,0:T(1,128)} %offsets_hbm.1, s32[1,16]{1,0:T(1,128)} %shifts_hbm.1, s32[1,16]{1,0:T(1,128)} %basis_ids_hbm.1, bf16[1,16]{1,0:T(2,128)(2,1)S(1)} %copy-done, ...), custom_call_target="tpu_custom_call" | custom-call | bytes 4194304 | tf_op jit(solution)/shard_map/own_terms/pallas_call | solution.py:304
  13.7 0.0 collective-permute-done.1.distant
  13.7 0.0 collective-permute-done.beside
  13.7 3.9 %mix.1 = (bf16[720,256]{1,0:T(8,128)(2,1)}, bf16[720,256]{1,0:T(8,128)(2,1)S(1)}, bf16[1024,256]{1,0:T(8,128)(2,1)}, f32[8,720,128]{2,1,0:T(8,128)S(1)}) custom-call(s32[1,128]{1,0:T(1,128)S(1)} %get-tuple-element.17.plan_in, f32[24,128]{1,0:T(8,128)S(1)} %get-tuple-element.18.coefs, ...), custom_call_target="tpu_custom_call", output_to_operand_aliasing={{3}: (4, {})} | custom-call | flops 754974720 | bytes 8388608 | tf_op jit(solution)/shard_map/mix/pallas_call | solution.py:334
  17.6 6.8 %all-to-all-start = ((bf16[64,16,256]{2,1,0:T(8,128)(2,1)}), bf16[64,16,256]{2,1,0:T(8,128)(2,1)S(1)}, u32[]{:S(2)}, u32[]{:S(2)}) async-start(bf16[64,16,256]{2,1,0:T(8,128)(2,1)} %bitcast.4), calls=%async_computation | async-start | bytes 1048576 | tf_op jit(solution)/shard_map/all_to_all | solution.py:405
  24.4 2.1 %backward.1 = (bf16[720,256]{1,0:T(8,128)(2,1)S(1)}, f32[720,256]{1,0:T(8,128)S(1)}, bf16[720,256]{1,0:T(8,128)(2,1)S(1)}) custom-call(s32[1,128]{1,0:T(1,128)S(1)} %get-tuple-element.17.plan_in, f32[24,128]{1,0:T(8,128)S(1)} %get-tuple-element.18.coefs, bf16[720,256]{1,0:T(8,128)(2,1)S(1)} %get-tuple-element.24.grad_pre, ...), custom_call_target="tpu_custom_call" | custom-call | flops 377487360 | bytes 8388608 | tf_op jit(solution)/shard_map/backward/pallas_call | solution.py:363
  26.6 3.6 %collective-permute-start.2 = (bf16[720,256]{1,0:T(8,128)(2,1)S(1)}, bf16[720,256]{1,0:T(8,128)(2,1)S(1)}, u32[]{:S(2)}, u32[]{:S(2)}) collective-permute-start(bf16[720,256]{1,0:T(8,128)(2,1)S(1)} %get-tuple-element.28), channel_id=1, source_target_pairs={{16,32},{48,64},{80,96},{112,128},{144,160},{176,192},{208,224},{2... | collective-permute-start | bytes 1105928 | tf_op jit(solution)/shard_map/ppermute | solution.py:409
  30.2 1.9 %collective-permute-start.3 = (bf16[720,256]{1,0:T(8,128)(2,1)S(1)}, bf16[720,256]{1,0:T(8,128)(2,1)S(1)}, u32[]{:S(2)}, u32[]{:S(2)}) collective-permute-start(bf16[720,256]{1,0:T(8,128)(2,1)S(1)} %get-tuple-element.25), channel_id=1, source_target_pairs={{0,16},{32,48},{64,80},{96,112},{128,144},{160,176},{192,208},{224... | collective-permute-start | bytes 1105928 | tf_op jit(solution)/shard_map/ppermute | solution.py:410
  32.1 3.9 %all-to-all-done = bf16[64,16,256]{2,1,0:T(8,128)(2,1)S(1)} async-done(((bf16[64,16,256]{2,1,0:T(8,128)(2,1)}), bf16[64,16,256]{2,1,0:T(8,128)(2,1)S(1)}, u32[]{:S(2)}, u32[]{:S(2)}) %all-to-all-start) | async-done | bytes 524320 | tf_op jit(solution)/shard_map/all_to_all | solution.py:405
  36.0 0.1 reduce_sum.21
  36.1 0.6 broadcast_in_dim.9
  36.7 14.3 %all-to-all-start.1 = ((bf16[8,16,256]{2,1,0:T(8,128)(2,1)}), bf16[8,16,256]{2,1,0:T(8,128)(2,1)S(1)}, u32[]{:S(2)}, u32[]{:S(2)}) async-start(bf16[8,16,256]{2,1,0:T(8,128)(2,1)} %broadcast_in_dim.9), calls=%async_computation.1 | async-start | bytes 131072 | tf_op jit(solution)/shard_map/all_to_all | solution.py:386
  51.0 0.0 collective-permute-done.2
  51.1 0.0 collective-permute-done.3
  51.1 0.8 %add_convert_fusion = bf16[720,256]{1,0:T(8,128)(2,1)} fusion(bf16[720,256]{1,0:T(8,128)(2,1)S(1)} %collective-permute-done.3, f32[720,256]{1,0:T(8,128)S(1)} %get-tuple-element.27, bf16[720,256]{1,0:T(8,128)(2,1)S(1)} %collective-permute-done.2), kind=kLoop, calls=%fused_computation | loop fusion | flops 921600 | bytes 1843200 | tf_op jit(solution)/shard_map/convert_element_type | solution.py:414
  51.9 12.1 %all-to-all-done.1 = bf16[8,16,256]{2,1,0:T(8,128)(2,1)S(1)} async-done(((bf16[8,16,256]{2,1,0:T(8,128)(2,1)}), bf16[8,16,256]{2,1,0:T(8,128)(2,1)S(1)}, u32[]{:S(2)}, u32[]{:S(2)}) %all-to-all-start.1) | async-done | bytes 65568 | tf_op jit(solution)/shard_map/all_to_all | solution.py:386
  64.1 17.7 %all_to_all.15 = bf16[64,16,256]{2,1,0:T(8,128)(2,1)S(1)} all-to-all(bf16[64,16,256]{2,1,0:T(8,128)(2,1)S(1)} %broadcast_in_dim.21), channel_id=1, replica_groups=mesh['za'=8,'zp'=2,'core'=2,'x'=4,'y'=4] {'zp','core','x','y'}, dimensions={0} | all-to-all | bytes 1048576 | tf_op jit(solution)/shard_map/all_to_all | solution.py:386
  81.8 1.1 %bitcast_convert_fusion = f32[4,256,256]{2,1,0:T(8,128)} fusion(bf16[4,256,256]{2,1,0:T(8,128)(2,1)S(1)} %bitcast.10), kind=kLoop, calls=%fused_computation.1 | loop fusion | flops 262144 | bytes 1572864 | tf_op jit(solution)/shard_map/convert_element_type | solution.py:419
  (3 shorter events, 0.1 us)
Async XLA Ops:
  0.6 13.1 %collective-permute-start.1 = (bf16[720,256]{1,0:T(8,128)(2,1)}, bf16[720,256]{1,0:T(8,128)(2,1)S(1)}, u32[]{:S(2)}, u32[]{:S(2)}) collective-permute-start(bf16[720,256]{1,0:T(8,128)(2,1)} %bitcast.14), channel_id=1, source_target_pairs={{16,32},{48,64},{80,96},{112,128},{144,160},{176,192},{208,224},{2... | collective-permute-start | bytes 1105928 | tf_op jit(solution)/shard_map/ppermute | solution.py:396
  5.6 8.2 %collective-permute-start = (bf16[720,256]{1,0:T(8,128)(2,1)}, bf16[720,256]{1,0:T(8,128)(2,1)S(1)}, u32[]{:S(2)}, u32[]{:S(2)}) collective-permute-start(bf16[720,256]{1,0:T(8,128)(2,1)} %bitcast.15), channel_id=1, source_target_pairs={{0,16},{32,48},{64,80},{96,112},{128,144},{160,176},{192,208},{224... | collective-permute-start | bytes 1105928 | tf_op jit(solution)/shard_map/ppermute | solution.py:397
  10.1 0.7 copy-start
  17.6 18.4 %all-to-all-start = ((bf16[64,16,256]{2,1,0:T(8,128)(2,1)}), bf16[64,16,256]{2,1,0:T(8,128)(2,1)S(1)}, u32[]{:S(2)}, u32[]{:S(2)}) async-start(bf16[64,16,256]{2,1,0:T(8,128)(2,1)} %bitcast.4), calls=%async_computation | async-start | bytes 1048576 | tf_op jit(solution)/shard_map/all_to_all | solution.py:405
  26.6 24.5 %collective-permute-start.2 = (bf16[720,256]{1,0:T(8,128)(2,1)S(1)}, bf16[720,256]{1,0:T(8,128)(2,1)S(1)}, u32[]{:S(2)}, u32[]{:S(2)}) collective-permute-start(bf16[720,256]{1,0:T(8,128)(2,1)S(1)} %get-tuple-element.28), channel_id=1, source_target_pairs={{16,32},{48,64},{80,96},{112,128},{144,160},{176,192},{208,224},{2... | collective-permute-start | bytes 1105928 | tf_op jit(solution)/shard_map/ppermute | solution.py:409
  30.2 20.9 %collective-permute-start.3 = (bf16[720,256]{1,0:T(8,128)(2,1)S(1)}, bf16[720,256]{1,0:T(8,128)(2,1)S(1)}, u32[]{:S(2)}, u32[]{:S(2)}) collective-permute-start(bf16[720,256]{1,0:T(8,128)(2,1)S(1)} %get-tuple-element.25), channel_id=1, source_target_pairs={{0,16},{32,48},{64,80},{96,112},{128,144},{160,176},{192,208},{224... | collective-permute-start | bytes 1105928 | tf_op jit(solution)/shard_map/ppermute | solution.py:410
  36.7 27.2 %all-to-all-start.1 = ((bf16[8,16,256]{2,1,0:T(8,128)(2,1)}), bf16[8,16,256]{2,1,0:T(8,128)(2,1)S(1)}, u32[]{:S(2)}, u32[]{:S(2)}) async-start(bf16[8,16,256]{2,1,0:T(8,128)(2,1)} %broadcast_in_dim.9), calls=%async_computation.1 | async-start | bytes 131072 | tf_op jit(solution)/shard_map/all_to_all | solution.py:386

commit v5 on v4

--- a/solution.py
+++ b/solution.py
@@ -21,7 +21,7 @@
 VMEM_BYTES = 48 * 1024 * 1024
 LAT = ("za", "zp", "core")
 ENS = ("x", "y")
-NEAR = ("zp", "core", "x", "y")
+NEAR = ("x", "y", "zp", "core")
 FAR = ("za",)
 
 

time: 83.3 us -> 84.8 us (1.018)
    all_to_all x1, waiting for transfers between devices: 3.93 us -> 5.2 us  [on_device(): lax.all_to_all(partial_w.reshape(lax.axis_size(NEAR), -1, channels), NEAR...]
  transfers between devices with their start and end apart: 6 -> 6, of which waited for: 2 -> 2; matrix products, arithmetic and copies ran while one was open for 2% -> 2% of each run, Pallas kernels for 6% -> 5%
where the time goes in v5:
time: 84.8 us; the launch traced here: 84.4 us
  starting transfers between devices  36.7 us (43%)
  blocking collectives  18.4 us (22%)
  waiting for transfers between devices  16.7 us (20%)
  Pallas kernels  8.53 us (10%)
  other arithmetic  2.03 us (2%)
  local copies, waits for them, and re-layouts  1.32 us (2%)
    all_to_all x1, blocking collectives, to_all(): lax.all_to_all(jnp.broadcast_to(block[None], (count,) + block.shape), axe...  18.4 us
    all_to_all x1, starting transfers between devices, to_all(): lax.all_to_all(jnp.broadcast_to(block[None], (count,) + block.shape), axe...  14.7 us
    all_to_all x1, waiting for transfers between devices, to_all(): lax.all_to_all(jnp.broadcast_to(block[None], (count,) + block.shape), axe...  11.5 us
    all_to_all x1, starting transfers between devices, on_device(): lax.all_to_all(partial_w.reshape(lax.axis_size(NEAR), -1, channels), NEAR...  6.9 us
    all_to_all x1, waiting for transfers between devices, on_device(): lax.all_to_all(partial_w.reshape(lax.axis_size(NEAR), -1, channels), NEAR...  5.2 us
    ppermute x1, starting transfers between devices, on_device(): distant = lax.ppermute(own, LAT, off_chip)  4.94 us
    ppermute x1, starting transfers between devices, on_device(): beside = lax.ppermute(own, LAT, on_chip)  4.54 us
    pallas_call x1, Pallas kernels, mix(): pl.pallas_call(mix_kernel, out_shape=(shape((lon_count, channels), BF16),...  4.06 us
  transfers between devices with their start and end apart: 6, of which 2 were waited for; matrix products, arithmetic and copies ran while one was open for 2% of the time, Pallas kernels for 5%

profile of v5, /device:TPU:1, one launch (start us, length us, event | category | flops | bytes accessed | tf_op | source)
XLA Modules:
  0.0 84.4 jit_solution(11583976192396189863)
XLA Ops:
  0.6 4.9 %collective-permute-start.1 = (bf16[720,256]{1,0:T(8,128)(2,1)}, bf16[720,256]{1,0:T(8,128)(2,1)S(1)}, u32[]{:S(2)}, u32[]{:S(2)}) collective-permute-start(bf16[720,256]{1,0:T(8,128)(2,1)} %bitcast.14), channel_id=1, source_target_pairs={{16,32},{48,64},{80,96},{112,128},{144,160},{176,192},{208,224},{2... | collective-permute-start | bytes 1105928 | tf_op jit(solution)/shard_map/ppermute | solution.py:396
  5.6 4.5 %collective-permute-start = (bf16[720,256]{1,0:T(8,128)(2,1)}, bf16[720,256]{1,0:T(8,128)(2,1)S(1)}, u32[]{:S(2)}, u32[]{:S(2)}) collective-permute-start(bf16[720,256]{1,0:T(8,128)(2,1)} %bitcast.15), channel_id=1, source_target_pairs={{0,16},{32,48},{64,80},{96,112},{128,144},{160,176},{192,208},{224... | collective-permute-start | bytes 1105928 | tf_op jit(solution)/shard_map/ppermute | solution.py:397
  10.1 0.0 copy-start
  10.1 0.6 copy-done
  10.8 2.5 %own_terms.1 = (f32[8,720,128]{2,1,0:T(8,128)S(1)}, f32[24,128]{1,0:T(8,128)S(1)}, s32[1,128]{1,0:T(1,128)S(1)}, bf16[1024,256]{1,0:T(8,128)(2,1)S(1)}, bf16[720,256]{1,0:T(8,128)(2,1)S(1)}) custom-call(s32[1,16]{1,0:T(1,128)} %offsets_hbm.1, s32[1,16]{1,0:T(1,128)} %shifts_hbm.1, s32[1,16]{1,0:T(1,128)} %basis_ids_hbm.1, bf16[1,16]{1,0:T(2,128)(2,1)S(1)} %copy-done, ...), custom_call_target="tpu_custom_call" | custom-call | bytes 4194304 | tf_op jit(solution)/shard_map/own_terms/pallas_call | solution.py:304
  13.3 0.0 collective-permute-done.1.distant
  13.3 0.0 collective-permute-done.beside
  13.3 4.1 %mix.1 = (bf16[720,256]{1,0:T(8,128)(2,1)}, bf16[720,256]{1,0:T(8,128)(2,1)S(1)}, bf16[1024,256]{1,0:T(8,128)(2,1)}, f32[8,720,128]{2,1,0:T(8,128)S(1)}) custom-call(s32[1,128]{1,0:T(1,128)S(1)} %get-tuple-element.17.plan_in, f32[24,128]{1,0:T(8,128)S(1)} %get-tuple-element.18.coefs, ...), custom_call_target="tpu_custom_call", output_to_operand_aliasing={{3}: (4, {})} | custom-call | flops 754974720 | bytes 8388608 | tf_op jit(solution)/shard_map/mix/pallas_call | solution.py:334
  17.4 6.9 %all-to-all-start = ((bf16[64,16,256]{2,1,0:T(8,128)(2,1)}), bf16[64,16,256]{2,1,0:T(8,128)(2,1)S(1)}, u32[]{:S(2)}, u32[]{:S(2)}) async-start(bf16[64,16,256]{2,1,0:T(8,128)(2,1)} %bitcast.4), calls=%async_computation | async-start | bytes 1048576 | tf_op jit(solution)/shard_map/all_to_all | solution.py:405
  24.3 2.0 %backward.1 = (bf16[720,256]{1,0:T(8,128)(2,1)S(1)}, f32[720,256]{1,0:T(8,128)S(1)}, bf16[720,256]{1,0:T(8,128)(2,1)S(1)}) custom-call(s32[1,128]{1,0:T(1,128)S(1)} %get-tuple-element.17.plan_in, f32[24,128]{1,0:T(8,128)S(1)} %get-tuple-element.18.coefs, bf16[720,256]{1,0:T(8,128)(2,1)S(1)} %get-tuple-element.24.grad_pre, ...), custom_call_target="tpu_custom_call" | custom-call | flops 377487360 | bytes 8388608 | tf_op jit(solution)/shard_map/backward/pallas_call | solution.py:363
  26.3 3.7 %collective-permute-start.2 = (bf16[720,256]{1,0:T(8,128)(2,1)S(1)}, bf16[720,256]{1,0:T(8,128)(2,1)S(1)}, u32[]{:S(2)}, u32[]{:S(2)}) collective-permute-start(bf16[720,256]{1,0:T(8,128)(2,1)S(1)} %get-tuple-element.28), channel_id=1, source_target_pairs={{16,32},{48,64},{80,96},{112,128},{144,160},{176,192},{208,224},{2... | collective-permute-start | bytes 1105928 | tf_op jit(solution)/shard_map/ppermute | solution.py:409
  29.9 1.9 %collective-permute-start.3 = (bf16[720,256]{1,0:T(8,128)(2,1)S(1)}, bf16[720,256]{1,0:T(8,128)(2,1)S(1)}, u32[]{:S(2)}, u32[]{:S(2)}) collective-permute-start(bf16[720,256]{1,0:T(8,128)(2,1)S(1)} %get-tuple-element.25), channel_id=1, source_target_pairs={{0,16},{32,48},{64,80},{96,112},{128,144},{160,176},{192,208},{224... | collective-permute-start | bytes 1105928 | tf_op jit(solution)/shard_map/ppermute | solution.py:410
  31.9 5.2 %all-to-all-done = bf16[64,16,256]{2,1,0:T(8,128)(2,1)S(1)} async-done(((bf16[64,16,256]{2,1,0:T(8,128)(2,1)}), bf16[64,16,256]{2,1,0:T(8,128)(2,1)S(1)}, u32[]{:S(2)}, u32[]{:S(2)}) %all-to-all-start) | async-done | bytes 524320 | tf_op jit(solution)/shard_map/all_to_all | solution.py:405
  37.1 0.1 reduce_sum.21
  37.2 0.6 broadcast_in_dim.9
  37.8 14.7 %all-to-all-start.1 = ((bf16[8,16,256]{2,1,0:T(8,128)(2,1)}), bf16[8,16,256]{2,1,0:T(8,128)(2,1)S(1)}, u32[]{:S(2)}, u32[]{:S(2)}) async-start(bf16[8,16,256]{2,1,0:T(8,128)(2,1)} %broadcast_in_dim.9), calls=%async_computation.1 | async-start | bytes 131072 | tf_op jit(solution)/shard_map/all_to_all | solution.py:386
  52.6 0.0 collective-permute-done.2
  52.6 0.0 collective-permute-done.3
  52.6 0.8 %add_convert_fusion = bf16[720,256]{1,0:T(8,128)(2,1)} fusion(bf16[720,256]{1,0:T(8,128)(2,1)S(1)} %collective-permute-done.3, f32[720,256]{1,0:T(8,128)S(1)} %get-tuple-element.27, bf16[720,256]{1,0:T(8,128)(2,1)S(1)} %collective-permute-done.2), kind=kLoop, calls=%fused_computation | loop fusion | flops 921600 | bytes 1843200 | tf_op jit(solution)/shard_map/convert_element_type | solution.py:414
  53.4 11.5 %all-to-all-done.1 = bf16[8,16,256]{2,1,0:T(8,128)(2,1)S(1)} async-done(((bf16[8,16,256]{2,1,0:T(8,128)(2,1)}), bf16[8,16,256]{2,1,0:T(8,128)(2,1)S(1)}, u32[]{:S(2)}, u32[]{:S(2)}) %all-to-all-start.1) | async-done | bytes 65568 | tf_op jit(solution)/shard_map/all_to_all | solution.py:386
  64.9 18.4 %all_to_all.15 = bf16[64,16,256]{2,1,0:T(8,128)(2,1)S(1)} all-to-all(bf16[64,16,256]{2,1,0:T(8,128)(2,1)S(1)} %broadcast_in_dim.21), channel_id=1, replica_groups=mesh['za'=8,'zp'=2,'core'=2,'x'=4,'y'=4] {'x','y','zp','core'}, dimensions={0} | all-to-all | bytes 1048576 | tf_op jit(solution)/shard_map/all_to_all | solution.py:386
  83.3 1.1 %bitcast_convert_fusion = f32[4,256,256]{2,1,0:T(8,128)} fusion(bf16[4,256,256]{2,1,0:T(8,128)(2,1)S(1)} %bitcast.10), kind=kLoop, calls=%fused_computation.1 | loop fusion | flops 262144 | bytes 1572864 | tf_op jit(solution)/shard_map/convert_element_type | solution.py:419
  (3 shorter events, 0.1 us)
Async XLA Ops:
  0.6 12.7 %collective-permute-start.1 = (bf16[720,256]{1,0:T(8,128)(2,1)}, bf16[720,256]{1,0:T(8,128)(2,1)S(1)}, u32[]{:S(2)}, u32[]{:S(2)}) collective-permute-start(bf16[720,256]{1,0:T(8,128)(2,1)} %bitcast.14), channel_id=1, source_target_pairs={{16,32},{48,64},{80,96},{112,128},{144,160},{176,192},{208,224},{2... | collective-permute-start | bytes 1105928 | tf_op jit(solution)/shard_map/ppermute | solution.py:396
  5.6 7.7 %collective-permute-start = (bf16[720,256]{1,0:T(8,128)(2,1)}, bf16[720,256]{1,0:T(8,128)(2,1)S(1)}, u32[]{:S(2)}, u32[]{:S(2)}) collective-permute-start(bf16[720,256]{1,0:T(8,128)(2,1)} %bitcast.15), channel_id=1, source_target_pairs={{0,16},{32,48},{64,80},{96,112},{128,144},{160,176},{192,208},{224... | collective-permute-start | bytes 1105928 | tf_op jit(solution)/shard_map/ppermute | solution.py:397
  10.1 0.7 copy-start
  17.4 19.7 %all-to-all-start = ((bf16[64,16,256]{2,1,0:T(8,128)(2,1)}), bf16[64,16,256]{2,1,0:T(8,128)(2,1)S(1)}, u32[]{:S(2)}, u32[]{:S(2)}) async-start(bf16[64,16,256]{2,1,0:T(8,128)(2,1)} %bitcast.4), calls=%async_computation | async-start | bytes 1048576 | tf_op jit(solution)/shard_map/all_to_all | solution.py:405
  26.3 26.3 %collective-permute-start.2 = (bf16[720,256]{1,0:T(8,128)(2,1)S(1)}, bf16[720,256]{1,0:T(8,128)(2,1)S(1)}, u32[]{:S(2)}, u32[]{:S(2)}) collective-permute-start(bf16[720,256]{1,0:T(8,128)(2,1)S(1)} %get-tuple-element.28), channel_id=1, source_target_pairs={{16,32},{48,64},{80,96},{112,128},{144,160},{176,192},{208,224},{2... | collective-permute-start | bytes 1105928 | tf_op jit(solution)/shard_map/ppermute | solution.py:409
  29.9 22.6 %collective-permute-start.3 = (bf16[720,256]{1,0:T(8,128)(2,1)S(1)}, bf16[720,256]{1,0:T(8,128)(2,1)S(1)}, u32[]{:S(2)}, u32[]{:S(2)}) collective-permute-start(bf16[720,256]{1,0:T(8,128)(2,1)S(1)} %get-tuple-element.25), channel_id=1, source_target_pairs={{0,16},{32,48},{64,80},{96,112},{128,144},{160,176},{192,208},{224... | collective-permute-start | bytes 1105928 | tf_op jit(solution)/shard_map/ppermute | solution.py:410
  37.8 27.1 %all-to-all-start.1 = ((bf16[8,16,256]{2,1,0:T(8,128)(2,1)}), bf16[8,16,256]{2,1,0:T(8,128)(2,1)S(1)}, u32[]{:S(2)}, u32[]{:S(2)}) async-start(bf16[8,16,256]{2,1,0:T(8,128)(2,1)} %broadcast_in_dim.9), calls=%async_computation.1 | async-start | bytes 131072 | tf_op jit(solution)/shard_map/all_to_all | solution.py:386

commit v6 on v5

--- a/solution.py
+++ b/solution.py
@@ -21,7 +21,7 @@
 VMEM_BYTES = 48 * 1024 * 1024
 LAT = ("za", "zp", "core")
 ENS = ("x", "y")
-NEAR = ("x", "y", "zp", "core")
+NEAR = ("core", "zp", "x", "y")
 FAR = ("za",)
 
 

time: 84.8 us -> 84.8 us (level)
  no operation moved by 1% of the time
where the time goes in v6:
time: 84.8 us; the launch traced here: 84.4 us
  starting transfers between devices  36.5 us (43%)
  blocking collectives  18.9 us (22%)
  waiting for transfers between devices  16.2 us (19%)
  Pallas kernels  8.74 us (10%)
  other arithmetic  2.03 us (2%)
  local copies, waits for them, and re-layouts  1.32 us (2%)
    all_to_all x1, blocking collectives, to_all(): lax.all_to_all(jnp.broadcast_to(block[None], (count,) + block.shape), axe...  18.9 us
    all_to_all x1, starting transfers between devices, to_all(): lax.all_to_all(jnp.broadcast_to(block[None], (count,) + block.shape), axe...  14.5 us
    all_to_all x1, waiting for transfers between devices, to_all(): lax.all_to_all(jnp.broadcast_to(block[None], (count,) + block.shape), axe...  11.1 us
    all_to_all x1, starting transfers between devices, on_device(): lax.all_to_all(partial_w.reshape(lax.axis_size(NEAR), -1, channels), NEAR...  6.92 us
    all_to_all x1, waiting for transfers between devices, on_device(): lax.all_to_all(partial_w.reshape(lax.axis_size(NEAR), -1, channels), NEAR...  5.09 us
    ppermute x1, starting transfers between devices, on_device(): distant = lax.ppermute(own, LAT, off_chip)  4.94 us
    ppermute x1, starting transfers between devices, on_device(): beside = lax.ppermute(own, LAT, on_chip)  4.54 us
    pallas_call x1, Pallas kernels, mix(): pl.pallas_call(mix_kernel, out_shape=(shape((lon_count, channels), BF16),...  4.27 us
  transfers between devices with their start and end apart: 6, of which 2 were waited for; matrix products, arithmetic and copies ran while one was open for 2% of the time, Pallas kernels for 5%

profile of v6, /device:TPU:1, one launch (start us, length us, event | category | flops | bytes accessed | tf_op | source)
XLA Modules:
  0.0 84.4 jit_solution(9271978823144505831)
XLA Ops:
  0.6 4.9 %collective-permute-start.1 = (bf16[720,256]{1,0:T(8,128)(2,1)}, bf16[720,256]{1,0:T(8,128)(2,1)S(1)}, u32[]{:S(2)}, u32[]{:S(2)}) collective-permute-start(bf16[720,256]{1,0:T(8,128)(2,1)} %bitcast.14), channel_id=1, source_target_pairs={{16,32},{48,64},{80,96},{112,128},{144,160},{176,192},{208,224},{2... | collective-permute-start | bytes 1105928 | tf_op jit(solution)/shard_map/ppermute | solution.py:396
  5.6 4.5 %collective-permute-start = (bf16[720,256]{1,0:T(8,128)(2,1)}, bf16[720,256]{1,0:T(8,128)(2,1)S(1)}, u32[]{:S(2)}, u32[]{:S(2)}) collective-permute-start(bf16[720,256]{1,0:T(8,128)(2,1)} %bitcast.15), channel_id=1, source_target_pairs={{0,16},{32,48},{64,80},{96,112},{128,144},{160,176},{192,208},{224... | collective-permute-start | bytes 1105928 | tf_op jit(solution)/shard_map/ppermute | solution.py:397
  10.1 0.0 copy-start
  10.1 0.6 copy-done
  10.8 2.6 %own_terms.1 = (f32[8,720,128]{2,1,0:T(8,128)S(1)}, f32[24,128]{1,0:T(8,128)S(1)}, s32[1,128]{1,0:T(1,128)S(1)}, bf16[1024,256]{1,0:T(8,128)(2,1)S(1)}, bf16[720,256]{1,0:T(8,128)(2,1)S(1)}) custom-call(s32[1,16]{1,0:T(1,128)} %offsets_hbm.1, s32[1,16]{1,0:T(1,128)} %shifts_hbm.1, s32[1,16]{1,0:T(1,128)} %basis_ids_hbm.1, bf16[1,16]{1,0:T(2,128)(2,1)S(1)} %copy-done, ...), custom_call_target="tpu_custom_call" | custom-call | bytes 4194304 | tf_op jit(solution)/shard_map/own_terms/pallas_call | solution.py:304
  13.4 0.0 collective-permute-done.1.distant
  13.4 0.0 collective-permute-done.beside
  13.4 4.3 %mix.1 = (bf16[720,256]{1,0:T(8,128)(2,1)}, bf16[720,256]{1,0:T(8,128)(2,1)S(1)}, bf16[1024,256]{1,0:T(8,128)(2,1)}, f32[8,720,128]{2,1,0:T(8,128)S(1)}) custom-call(s32[1,128]{1,0:T(1,128)S(1)} %get-tuple-element.17.plan_in, f32[24,128]{1,0:T(8,128)S(1)} %get-tuple-element.18.coefs, ...), custom_call_target="tpu_custom_call", output_to_operand_aliasing={{3}: (4, {})} | custom-call | flops 754974720 | bytes 8388608 | tf_op jit(solution)/shard_map/mix/pallas_call | solution.py:334
  17.7 6.9 %all-to-all-start = ((bf16[64,16,256]{2,1,0:T(8,128)(2,1)}), bf16[64,16,256]{2,1,0:T(8,128)(2,1)S(1)}, u32[]{:S(2)}, u32[]{:S(2)}) async-start(bf16[64,16,256]{2,1,0:T(8,128)(2,1)} %bitcast.4), calls=%async_computation | async-start | bytes 1048576 | tf_op jit(solution)/shard_map/all_to_all | solution.py:405
  24.6 1.9 %backward.1 = (bf16[720,256]{1,0:T(8,128)(2,1)S(1)}, f32[720,256]{1,0:T(8,128)S(1)}, bf16[720,256]{1,0:T(8,128)(2,1)S(1)}) custom-call(s32[1,128]{1,0:T(1,128)S(1)} %get-tuple-element.17.plan_in, f32[24,128]{1,0:T(8,128)S(1)} %get-tuple-element.18.coefs, bf16[720,256]{1,0:T(8,128)(2,1)S(1)} %get-tuple-element.24.grad_pre, ...), custom_call_target="tpu_custom_call" | custom-call | flops 377487360 | bytes 8388608 | tf_op jit(solution)/shard_map/backward/pallas_call | solution.py:363
  26.5 3.7 %collective-permute-start.2 = (bf16[720,256]{1,0:T(8,128)(2,1)S(1)}, bf16[720,256]{1,0:T(8,128)(2,1)S(1)}, u32[]{:S(2)}, u32[]{:S(2)}) collective-permute-start(bf16[720,256]{1,0:T(8,128)(2,1)S(1)} %get-tuple-element.28), channel_id=1, source_target_pairs={{16,32},{48,64},{80,96},{112,128},{144,160},{176,192},{208,224},{2... | collective-permute-start | bytes 1105928 | tf_op jit(solution)/shard_map/ppermute | solution.py:409
  30.2 1.9 %collective-permute-start.3 = (bf16[720,256]{1,0:T(8,128)(2,1)S(1)}, bf16[720,256]{1,0:T(8,128)(2,1)S(1)}, u32[]{:S(2)}, u32[]{:S(2)}) collective-permute-start(bf16[720,256]{1,0:T(8,128)(2,1)S(1)} %get-tuple-element.25), channel_id=1, source_target_pairs={{0,16},{32,48},{64,80},{96,112},{128,144},{160,176},{192,208},{224... | collective-permute-start | bytes 1105928 | tf_op jit(solution)/shard_map/ppermute | solution.py:410
  32.1 5.1 %all-to-all-done = bf16[64,16,256]{2,1,0:T(8,128)(2,1)S(1)} async-done(((bf16[64,16,256]{2,1,0:T(8,128)(2,1)}), bf16[64,16,256]{2,1,0:T(8,128)(2,1)S(1)}, u32[]{:S(2)}, u32[]{:S(2)}) %all-to-all-start) | async-done | bytes 524320 | tf_op jit(solution)/shard_map/all_to_all | solution.py:405
  37.2 0.1 reduce_sum.21
  37.3 0.6 broadcast_in_dim.9
  37.9 14.5 %all-to-all-start.1 = ((bf16[8,16,256]{2,1,0:T(8,128)(2,1)}), bf16[8,16,256]{2,1,0:T(8,128)(2,1)S(1)}, u32[]{:S(2)}, u32[]{:S(2)}) async-start(bf16[8,16,256]{2,1,0:T(8,128)(2,1)} %broadcast_in_dim.9), calls=%async_computation.1 | async-start | bytes 131072 | tf_op jit(solution)/shard_map/all_to_all | solution.py:386
  52.4 0.0 collective-permute-done.2
  52.4 0.0 collective-permute-done.3
  52.4 0.8 %add_convert_fusion = bf16[720,256]{1,0:T(8,128)(2,1)} fusion(bf16[720,256]{1,0:T(8,128)(2,1)S(1)} %collective-permute-done.3, f32[720,256]{1,0:T(8,128)S(1)} %get-tuple-element.27, bf16[720,256]{1,0:T(8,128)(2,1)S(1)} %collective-permute-done.2), kind=kLoop, calls=%fused_computation | loop fusion | flops 921600 | bytes 1843200 | tf_op jit(solution)/shard_map/convert_element_type | solution.py:414
  53.3 11.1 %all-to-all-done.1 = bf16[8,16,256]{2,1,0:T(8,128)(2,1)S(1)} async-done(((bf16[8,16,256]{2,1,0:T(8,128)(2,1)}), bf16[8,16,256]{2,1,0:T(8,128)(2,1)S(1)}, u32[]{:S(2)}, u32[]{:S(2)}) %all-to-all-start.1) | async-done | bytes 65568 | tf_op jit(solution)/shard_map/all_to_all | solution.py:386
  64.4 18.9 %all_to_all.15 = bf16[64,16,256]{2,1,0:T(8,128)(2,1)S(1)} all-to-all(bf16[64,16,256]{2,1,0:T(8,128)(2,1)S(1)} %broadcast_in_dim.21), channel_id=1, replica_groups=mesh['za'=8,'zp'=2,'core'=2,'x'=4,'y'=4] {'core','zp','x','y'}, dimensions={0} | all-to-all | bytes 1048576 | tf_op jit(solution)/shard_map/all_to_all | solution.py:386
  83.3 1.1 %bitcast_convert_fusion = f32[4,256,256]{2,1,0:T(8,128)} fusion(bf16[4,256,256]{2,1,0:T(8,128)(2,1)S(1)} %bitcast.10), kind=kLoop, calls=%fused_computation.1 | loop fusion | flops 262144 | bytes 1572864 | tf_op jit(solution)/shard_map/convert_element_type | solution.py:419
  (3 shorter events, 0.1 us)
Async XLA Ops:
  0.6 12.8 %collective-permute-start.1 = (bf16[720,256]{1,0:T(8,128)(2,1)}, bf16[720,256]{1,0:T(8,128)(2,1)S(1)}, u32[]{:S(2)}, u32[]{:S(2)}) collective-permute-start(bf16[720,256]{1,0:T(8,128)(2,1)} %bitcast.14), channel_id=1, source_target_pairs={{16,32},{48,64},{80,96},{112,128},{144,160},{176,192},{208,224},{2... | collective-permute-start | bytes 1105928 | tf_op jit(solution)/shard_map/ppermute | solution.py:396
  5.6 7.8 %collective-permute-start = (bf16[720,256]{1,0:T(8,128)(2,1)}, bf16[720,256]{1,0:T(8,128)(2,1)S(1)}, u32[]{:S(2)}, u32[]{:S(2)}) collective-permute-start(bf16[720,256]{1,0:T(8,128)(2,1)} %bitcast.15), channel_id=1, source_target_pairs={{0,16},{32,48},{64,80},{96,112},{128,144},{160,176},{192,208},{224... | collective-permute-start | bytes 1105928 | tf_op jit(solution)/shard_map/ppermute | solution.py:397
  10.1 0.7 copy-start
  17.7 19.5 %all-to-all-start = ((bf16[64,16,256]{2,1,0:T(8,128)(2,1)}), bf16[64,16,256]{2,1,0:T(8,128)(2,1)S(1)}, u32[]{:S(2)}, u32[]{:S(2)}) async-start(bf16[64,16,256]{2,1,0:T(8,128)(2,1)} %bitcast.4), calls=%async_computation | async-start | bytes 1048576 | tf_op jit(solution)/shard_map/all_to_all | solution.py:405
  26.5 25.9 %collective-permute-start.2 = (bf16[720,256]{1,0:T(8,128)(2,1)S(1)}, bf16[720,256]{1,0:T(8,128)(2,1)S(1)}, u32[]{:S(2)}, u32[]{:S(2)}) collective-permute-start(bf16[720,256]{1,0:T(8,128)(2,1)S(1)} %get-tuple-element.28), channel_id=1, source_target_pairs={{16,32},{48,64},{80,96},{112,128},{144,160},{176,192},{208,224},{2... | collective-permute-start | bytes 1105928 | tf_op jit(solution)/shard_map/ppermute | solution.py:409
  30.2 22.3 %collective-permute-start.3 = (bf16[720,256]{1,0:T(8,128)(2,1)S(1)}, bf16[720,256]{1,0:T(8,128)(2,1)S(1)}, u32[]{:S(2)}, u32[]{:S(2)}) collective-permute-start(bf16[720,256]{1,0:T(8,128)(2,1)S(1)} %get-tuple-element.25), channel_id=1, source_target_pairs={{0,16},{32,48},{64,80},{96,112},{128,144},{160,176},{192,208},{224... | collective-permute-start | bytes 1105928 | tf_op jit(solution)/shard_map/ppermute | solution.py:410
  37.9 26.4 %all-to-all-start.1 = ((bf16[8,16,256]{2,1,0:T(8,128)(2,1)}), bf16[8,16,256]{2,1,0:T(8,128)(2,1)S(1)}, u32[]{:S(2)}, u32[]{:S(2)}) async-start(bf16[8,16,256]{2,1,0:T(8,128)(2,1)} %broadcast_in_dim.9), calls=%async_computation.1 | async-start | bytes 131072 | tf_op jit(solution)/shard_map/all_to_all | solution.py:386

commit v7 on v6

--- a/solution.py
+++ b/solution.py
@@ -21,7 +21,7 @@
 VMEM_BYTES = 48 * 1024 * 1024
 LAT = ("za", "zp", "core")
 ENS = ("x", "y")
-NEAR = ("core", "zp", "x", "y")
+NEAR = ("zp", "core", "y", "x")
 FAR = ("za",)
 
 

time: 84.8 us -> 83.5 us (0.985)
  blocking collectives: 18.9 us -> 17.9 us
    all_to_all x1, waiting for transfers between devices: 5.09 us -> 3.67 us  [on_device(): lax.all_to_all(partial_w.reshape(lax.axis_size(NEAR), -1, channels), NEAR...]
    all_to_all x1, blocking collectives: 18.9 us -> 17.9 us  [to_all(): lax.all_to_all(jnp.broadcast_to(block[None], (count,) + block.shape), axe...]
    all_to_all x1, waiting for transfers between devices: 11.1 us -> 11.9 us  [to_all(): lax.all_to_all(jnp.broadcast_to(block[None], (count,) + block.shape), axe...]
  transfers between devices with their start and end apart: 6 -> 6, of which waited for: 2 -> 2; matrix products, arithmetic and copies ran while one was open for 2% -> 2% of each run, Pallas kernels for 5% -> 6%
where the time goes in v7:
time: 83.5 us; the launch traced here: 83.2 us
  starting transfers between devices  36.6 us (44%)
  blocking collectives  17.9 us (21%)
  waiting for transfers between devices  15.6 us (19%)
  Pallas kernels  8.93 us (11%)
  other arithmetic  2.03 us (2%)
  local copies, waits for them, and re-layouts  1.32 us (2%)
    all_to_all x1, blocking collectives, to_all(): lax.all_to_all(jnp.broadcast_to(block[None], (count,) + block.shape), axe...  17.9 us
    all_to_all x1, starting transfers between devices, to_all(): lax.all_to_all(jnp.broadcast_to(block[None], (count,) + block.shape), axe...  14.4 us
    all_to_all x1, waiting for transfers between devices, to_all(): lax.all_to_all(jnp.broadcast_to(block[None], (count,) + block.shape), axe...  11.9 us
    all_to_all x1, starting transfers between devices, on_device(): lax.all_to_all(partial_w.reshape(lax.axis_size(NEAR), -1, channels), NEAR...  7.02 us
    ppermute x1, starting transfers between devices, on_device(): distant = lax.ppermute(own, LAT, off_chip)  4.94 us
    ppermute x1, starting transfers between devices, on_device(): beside = lax.ppermute(own, LAT, on_chip)  4.54 us
    pallas_call x1, Pallas kernels, mix(): pl.pallas_call(mix_kernel, out_shape=(shape((lon_count, channels), BF16),...  4.09 us
    ppermute x1, starting transfers between devices, on_device(): from_distant = lax.ppermute(to_distant, LAT, off_chip)  3.81 us
  transfers between devices with their start and end apart: 6, of which 2 were waited for; matrix products, arithmetic and copies ran while one was open for 2% of the time, Pallas kernels for 6%

profile of v7, /device:TPU:1, one launch (start us, length us, event | category | flops | bytes accessed | tf_op | source)
XLA Modules:
  0.0 83.2 jit_solution(8157330970283983680)
XLA Ops:
  0.6 4.9 %collective-permute-start.1 = (bf16[720,256]{1,0:T(8,128)(2,1)}, bf16[720,256]{1,0:T(8,128)(2,1)S(1)}, u32[]{:S(2)}, u32[]{:S(2)}) collective-permute-start(bf16[720,256]{1,0:T(8,128)(2,1)} %bitcast.14), channel_id=1, source_target_pairs={{16,32},{48,64},{80,96},{112,128},{144,160},{176,192},{208,224},{2... | collective-permute-start | bytes 1105928 | tf_op jit(solution)/shard_map/ppermute | solution.py:396
  5.6 4.5 %collective-permute-start = (bf16[720,256]{1,0:T(8,128)(2,1)}, bf16[720,256]{1,0:T(8,128)(2,1)S(1)}, u32[]{:S(2)}, u32[]{:S(2)}) collective-permute-start(bf16[720,256]{1,0:T(8,128)(2,1)} %bitcast.15), channel_id=1, source_target_pairs={{0,16},{32,48},{64,80},{96,112},{128,144},{160,176},{192,208},{224... | collective-permute-start | bytes 1105928 | tf_op jit(solution)/shard_map/ppermute | solution.py:397
  10.1 0.0 copy-start
  10.1 0.6 copy-done
  10.8 2.7 %own_terms.1 = (f32[8,720,128]{2,1,0:T(8,128)S(1)}, f32[24,128]{1,0:T(8,128)S(1)}, s32[1,128]{1,0:T(1,128)S(1)}, bf16[1024,256]{1,0:T(8,128)(2,1)S(1)}, bf16[720,256]{1,0:T(8,128)(2,1)S(1)}) custom-call(s32[1,16]{1,0:T(1,128)} %offsets_hbm.1, s32[1,16]{1,0:T(1,128)} %shifts_hbm.1, s32[1,16]{1,0:T(1,128)} %basis_ids_hbm.1, bf16[1,16]{1,0:T(2,128)(2,1)S(1)} %copy-done, ...), custom_call_target="tpu_custom_call" | custom-call | bytes 4194304 | tf_op jit(solution)/shard_map/own_terms/pallas_call | solution.py:304
  13.5 0.0 collective-permute-done.1.distant
  13.5 0.0 collective-permute-done.beside
  13.5 4.1 %mix.1 = (bf16[720,256]{1,0:T(8,128)(2,1)}, bf16[720,256]{1,0:T(8,128)(2,1)S(1)}, bf16[1024,256]{1,0:T(8,128)(2,1)}, f32[8,720,128]{2,1,0:T(8,128)S(1)}) custom-call(s32[1,128]{1,0:T(1,128)S(1)} %get-tuple-element.17.plan_in, f32[24,128]{1,0:T(8,128)S(1)} %get-tuple-element.18.coefs, ...), custom_call_target="tpu_custom_call", output_to_operand_aliasing={{3}: (4, {})} | custom-call | flops 754974720 | bytes 8388608 | tf_op jit(solution)/shard_map/mix/pallas_call | solution.py:334
  17.6 7.0 %all-to-all-start = ((bf16[64,16,256]{2,1,0:T(8,128)(2,1)}), bf16[64,16,256]{2,1,0:T(8,128)(2,1)S(1)}, u32[]{:S(2)}, u32[]{:S(2)}) async-start(bf16[64,16,256]{2,1,0:T(8,128)(2,1)} %bitcast.4), calls=%async_computation | async-start | bytes 1048576 | tf_op jit(solution)/shard_map/all_to_all | solution.py:405
  24.6 2.2 %backward.1 = (bf16[720,256]{1,0:T(8,128)(2,1)S(1)}, f32[720,256]{1,0:T(8,128)S(1)}, bf16[720,256]{1,0:T(8,128)(2,1)S(1)}) custom-call(s32[1,128]{1,0:T(1,128)S(1)} %get-tuple-element.17.plan_in, f32[24,128]{1,0:T(8,128)S(1)} %get-tuple-element.18.coefs, bf16[720,256]{1,0:T(8,128)(2,1)S(1)} %get-tuple-element.24.grad_pre, ...), custom_call_target="tpu_custom_call" | custom-call | flops 377487360 | bytes 8388608 | tf_op jit(solution)/shard_map/backward/pallas_call | solution.py:363
  26.8 3.8 %collective-permute-start.2 = (bf16[720,256]{1,0:T(8,128)(2,1)S(1)}, bf16[720,256]{1,0:T(8,128)(2,1)S(1)}, u32[]{:S(2)}, u32[]{:S(2)}) collective-permute-start(bf16[720,256]{1,0:T(8,128)(2,1)S(1)} %get-tuple-element.28), channel_id=1, source_target_pairs={{16,32},{48,64},{80,96},{112,128},{144,160},{176,192},{208,224},{2... | collective-permute-start | bytes 1105928 | tf_op jit(solution)/shard_map/ppermute | solution.py:409
  30.6 1.9 %collective-permute-start.3 = (bf16[720,256]{1,0:T(8,128)(2,1)S(1)}, bf16[720,256]{1,0:T(8,128)(2,1)S(1)}, u32[]{:S(2)}, u32[]{:S(2)}) collective-permute-start(bf16[720,256]{1,0:T(8,128)(2,1)S(1)} %get-tuple-element.25), channel_id=1, source_target_pairs={{0,16},{32,48},{64,80},{96,112},{128,144},{160,176},{192,208},{224... | collective-permute-start | bytes 1105928 | tf_op jit(solution)/shard_map/ppermute | solution.py:410
  32.5 3.7 %all-to-all-done = bf16[64,16,256]{2,1,0:T(8,128)(2,1)S(1)} async-done(((bf16[64,16,256]{2,1,0:T(8,128)(2,1)}), bf16[64,16,256]{2,1,0:T(8,128)(2,1)S(1)}, u32[]{:S(2)}, u32[]{:S(2)}) %all-to-all-start) | async-done | bytes 524320 | tf_op jit(solution)/shard_map/all_to_all | solution.py:405
  36.2 0.1 reduce_sum.21
  36.3 0.6 broadcast_in_dim.9
  36.9 14.4 %all-to-all-start.1 = ((bf16[8,16,256]{2,1,0:T(8,128)(2,1)}), bf16[8,16,256]{2,1,0:T(8,128)(2,1)S(1)}, u32[]{:S(2)}, u32[]{:S(2)}) async-start(bf16[8,16,256]{2,1,0:T(8,128)(2,1)} %broadcast_in_dim.9), calls=%async_computation.1 | async-start | bytes 131072 | tf_op jit(solution)/shard_map/all_to_all | solution.py:386
  51.3 0.0 collective-permute-done.2
  51.3 0.0 collective-permute-done.3
  51.3 0.8 %add_convert_fusion = bf16[720,256]{1,0:T(8,128)(2,1)} fusion(bf16[720,256]{1,0:T(8,128)(2,1)S(1)} %collective-permute-done.3, f32[720,256]{1,0:T(8,128)S(1)} %get-tuple-element.27, bf16[720,256]{1,0:T(8,128)(2,1)S(1)} %collective-permute-done.2), kind=kLoop, calls=%fused_computation | loop fusion | flops 921600 | bytes 1843200 | tf_op jit(solution)/shard_map/convert_element_type | solution.py:414
  52.2 11.9 %all-to-all-done.1 = bf16[8,16,256]{2,1,0:T(8,128)(2,1)S(1)} async-done(((bf16[8,16,256]{2,1,0:T(8,128)(2,1)}), bf16[8,16,256]{2,1,0:T(8,128)(2,1)S(1)}, u32[]{:S(2)}, u32[]{:S(2)}) %all-to-all-start.1) | async-done | bytes 65568 | tf_op jit(solution)/shard_map/all_to_all | solution.py:386
  64.2 17.9 %all_to_all.15 = bf16[64,16,256]{2,1,0:T(8,128)(2,1)S(1)} all-to-all(bf16[64,16,256]{2,1,0:T(8,128)(2,1)S(1)} %broadcast_in_dim.21), channel_id=1, replica_groups=mesh['za'=8,'zp'=2,'core'=2,'x'=4,'y'=4] {'zp','core','y','x'}, dimensions={0} | all-to-all | bytes 1048576 | tf_op jit(solution)/shard_map/all_to_all | solution.py:386
  82.1 1.1 %bitcast_convert_fusion = f32[4,256,256]{2,1,0:T(8,128)} fusion(bf16[4,256,256]{2,1,0:T(8,128)(2,1)S(1)} %bitcast.10), kind=kLoop, calls=%fused_computation.1 | loop fusion | flops 262144 | bytes 1572864 | tf_op jit(solution)/shard_map/convert_element_type | solution.py:419
  (3 shorter events, 0.1 us)
Async XLA Ops:
  0.6 12.8 %collective-permute-start.1 = (bf16[720,256]{1,0:T(8,128)(2,1)}, bf16[720,256]{1,0:T(8,128)(2,1)S(1)}, u32[]{:S(2)}, u32[]{:S(2)}) collective-permute-start(bf16[720,256]{1,0:T(8,128)(2,1)} %bitcast.14), channel_id=1, source_target_pairs={{16,32},{48,64},{80,96},{112,128},{144,160},{176,192},{208,224},{2... | collective-permute-start | bytes 1105928 | tf_op jit(solution)/shard_map/ppermute | solution.py:396
  5.6 7.9 %collective-permute-start = (bf16[720,256]{1,0:T(8,128)(2,1)}, bf16[720,256]{1,0:T(8,128)(2,1)S(1)}, u32[]{:S(2)}, u32[]{:S(2)}) collective-permute-start(bf16[720,256]{1,0:T(8,128)(2,1)} %bitcast.15), channel_id=1, source_target_pairs={{0,16},{32,48},{64,80},{96,112},{128,144},{160,176},{192,208},{224... | collective-permute-start | bytes 1105928 | tf_op jit(solution)/shard_map/ppermute | solution.py:397
  10.1 0.7 copy-start
  17.6 18.6 %all-to-all-start = ((bf16[64,16,256]{2,1,0:T(8,128)(2,1)}), bf16[64,16,256]{2,1,0:T(8,128)(2,1)S(1)}, u32[]{:S(2)}, u32[]{:S(2)}) async-start(bf16[64,16,256]{2,1,0:T(8,128)(2,1)} %bitcast.4), calls=%async_computation | async-start | bytes 1048576 | tf_op jit(solution)/shard_map/all_to_all | solution.py:405
  26.8 24.6 %collective-permute-start.2 = (bf16[720,256]{1,0:T(8,128)(2,1)S(1)}, bf16[720,256]{1,0:T(8,128)(2,1)S(1)}, u32[]{:S(2)}, u32[]{:S(2)}) collective-permute-start(bf16[720,256]{1,0:T(8,128)(2,1)S(1)} %get-tuple-element.28), channel_id=1, source_target_pairs={{16,32},{48,64},{80,96},{112,128},{144,160},{176,192},{208,224},{2... | collective-permute-start | bytes 1105928 | tf_op jit(solution)/shard_map/ppermute | solution.py:409
  30.6 20.7 %collective-permute-start.3 = (bf16[720,256]{1,0:T(8,128)(2,1)S(1)}, bf16[720,256]{1,0:T(8,128)(2,1)S(1)}, u32[]{:S(2)}, u32[]{:S(2)}) collective-permute-start(bf16[720,256]{1,0:T(8,128)(2,1)S(1)} %get-tuple-element.25), channel_id=1, source_target_pairs={{0,16},{32,48},{64,80},{96,112},{128,144},{160,176},{192,208},{224... | collective-permute-start | bytes 1105928 | tf_op jit(solution)/shard_map/ppermute | solution.py:410
  36.9 27.2 %all-to-all-start.1 = ((bf16[8,16,256]{2,1,0:T(8,128)(2,1)}), bf16[8,16,256]{2,1,0:T(8,128)(2,1)S(1)}, u32[]{:S(2)}, u32[]{:S(2)}) async-start(bf16[8,16,256]{2,1,0:T(8,128)(2,1)} %broadcast_in_dim.9), calls=%async_computation.1 | async-start | bytes 131072 | tf_op jit(solution)/shard_map/all_to_all | solution.py:386
